TPU v7x, 256 devices: a whole 4x4x8 slice. The times are simulated.
256 devices in a mesh: dom: 256 (over y, z, x, core).
Axes of the slice: x: 4, y: 4, z: 8, core: 2. Of those that a mesh axis runs over, the one named last changes fastest.
Arguments:
- right_side: float32 [16384, 32, 64], P('dom'), as said below
- a_blocks: float32 [16384, 7, 64, 64], P('dom'), as said below
- a_cols: int32 [16384, 6], P('dom'), may hold values from 0 to 95, as said below
- g_blocks: float32 [16384, 4, 64, 64], P('dom'), as said below
- g_cols: int32 [16384, 3], P('dom'), may hold values from 0 to 79, as said below
- send_up: int32 [256, 16], P('dom'), may hold values from 0 to 63, as said below
- send_down: int32 [256, 16], P('dom'), may hold values from 0 to 63, as said below
Outputs:
- solution: float32 [16384, 32, 64], P('dom')
- residual: float32 [16384, 32, 64], P('dom')
Inputs may be any that keep to these rules, and one draw needn't show every extreme that they name: `a_cols`: neighbour columns of each block row in the order -x, +x, -y, +y, -z, +z of a periodic element grid: a value below 64 is an own block, 64 + h the h-th block from the device below, 80 + h the h-th block from the device above. `g_cols`: the -x, -y and -z columns of a_cols of the same row; a column is 64 or more exactly on the rows listed in send_down, and those rows' other columns are rows listed in send_down. `send_up`: for each device, 16 different local block indices. `send_down`: for each device, 16 different local block indices. `a_blocks`: the matrix is symmetric and positive definite: the couplings of two neighbouring rows are transposes of each other. `g_blocks`: the factor is nonsingular. `right_side`: Right-hand sides.
All inputs are finite; a program needn't handle non-finite values.
Results may differ from a plain program's by a relative error of at most 0.0005.
Values sent between devices are 32-bit elements; how exact they have to be, the bound alone decides.
A program may use at most 128 MiB of HBM per device.

v0:
```python
import jax
import jax.numpy as jnp
from jax import lax
from jax.sharding import PartitionSpec as P

ITERS = 3


HIGH = lax.Precision.HIGHEST


def padded_2(block, sides, width):
    for axis, dim in sides:
        count = lax.axis_size(axis)
        forward = [(i, i + 1) for i in range(count - 1)]
        forward.append((count - 1, 0))
        backward = [(target, source) for source, target in forward]
        low = lax.ppermute(
            lax.slice_in_dim(block, block.shape[dim] - width, None, axis=dim), axis, forward
        )
        high = lax.ppermute(lax.slice_in_dim(block, 0, width, axis=dim), axis, backward)
        block = jnp.concatenate([low, block, high], axis=dim)
    return block


def shifted(value, axis, steps):
    count = lax.axis_size(axis)
    pairs = [(source, (source + steps) % count) for source in range(count)]
    return lax.ppermute(value, axis, pairs)


def block_product(diag_blocks, off_blocks, columns, extended, own_field):
    own_part = jnp.einsum("nab,nrb->nra", diag_blocks, own_field, precision=HIGH)
    nearby = extended[columns]
    return own_part + jnp.einsum("nkab,nkrb->nra", off_blocks, nearby, precision=HIGH)


def inner_product(first, second):
    return jnp.sum(first * second, axis=(0, 2))


def residual_norm(residual, precond):
    return lax.psum(inner_product(residual, precond), "dom")


def body(right_side, a_blocks, a_cols, g_blocks, g_cols, send_up, send_down):
    upper = send_up[0]
    lower = send_down[0]
    local_rows = right_side.shape[0]
    face_rows = upper.shape[0]
    a_diagonal = a_blocks[:, 0]
    a_offdiag = a_blocks[:, 1:]
    g_diagonal = g_blocks[:, 0]
    g_offdiag = g_blocks[:, 1:]

    def precondition(field):
        received = shifted(field[upper], "dom", 1)
        extended = jnp.concatenate([field, received], axis=0)
        values = block_product(g_diagonal, g_offdiag, g_cols, extended, field)
        own_part = jnp.einsum("nab,nra->nrb", g_diagonal, values, precision=HIGH)
        partial_terms = jnp.einsum("nkab,nra->nkrb", g_offdiag, values, precision=HIGH)
        buffer = jax.ops.segment_sum(
            partial_terms.reshape(-1, values.shape[1], values.shape[2]),
            g_cols.reshape(-1),
            num_segments=local_rows + face_rows,
        )
        returned = shifted(buffer[local_rows:], "dom", -1)
        return (own_part + buffer[:local_rows]).at[upper].add(returned)

    solution = jnp.zeros_like(right_side)
    residual = right_side
    precond = precondition(residual)
    rz_now = residual_norm(residual, precond)
    direction = precond
    for iteration in range(ITERS):
        stacked = jnp.concatenate([direction[lower], direction[upper]], axis=0)
        padded = padded_2(stacked, (("dom", 0),), face_rows)
        operate_extended = jnp.concatenate(
            [direction, padded[:face_rows], padded[3 * face_rows :]], axis=0
        )
        image = block_product(a_diagonal, a_offdiag, a_cols, operate_extended, direction)
        alpha = rz_now / lax.psum(inner_product(direction, image), "dom")
        solution = solution + alpha[None, :, None] * direction
        residual = residual - alpha[None, :, None] * image
        if iteration + 1 < ITERS:
            precond = precondition(residual)
            rz_next = residual_norm(residual, precond)
            direction = precond + (rz_next / rz_now)[None, :, None] * direction
            rz_now = rz_next
    return (solution, residual)


def solution(mesh):
    in_specs = (
        P("dom", None, None),
        P("dom", None, None, None),
        P("dom", None),
        P("dom", None, None, None),
        P("dom", None),
        P("dom", None),
        P("dom", None),
    )
    out_specs = (P("dom", None, None), P("dom", None, None))
    return jax.shard_map(body, mesh=mesh, in_specs=in_specs, out_specs=out_specs, check_vma=False)
```

profile of v0, /device:TPU:1, one launch (start us, length us, event | category | flops | bytes accessed | tf_op | source)
XLA Modules:
  0.0 721.3 jit_solution(9972357921826656043)
XLA Ops:
  13.0 9.5 %fusion.72 = f32[64,32,64]{2,1,0:T(8,128)S(1)} fusion(f32[64,3,32,64]{3,2,1,0:T(8,128)} %bitcast.126, f32[64,4,64,64]{3,2,1,0:T(8,128)} %param.10), kind=kOutput, calls=%fused_computation.78 | convolution fusion | flops 301989888 | bytes 9961472 | tf_op jit(solution)/shard_map/nkab,nkrb->nra/dot_general | solution.py:35
  27.5 7.3 %fusion.14 = f32[64,32,3,64]{3,1,2,0:T(8,128)} fusion(f32[64,4,64,64]{3,2,1,0:T(8,128)} %param.10, f32[64,32,64]{2,1,0:T(8,128)S(1)} %fusion.45), kind=kOutput, calls=%fused_computation.35 | convolution fusion | flops 301989888 | bytes 8388608 | tf_op jit(solution)/shard_map/nkab,nra->nkrb/dot_general | solution.py:61
  35.0 17.3 %scatter_fusion = f32[80,32,64]{2,1,0:T(8,128)S(1)} fusion(f32[80,32,64]{2,1,0:T(8,128)S(1)} %broadcast.58.clone, s32[192]{0:T(256)S(1)} %reshape.199, f32[192,32,64]{2,1,0:T(8,128)} %bitcast.123), kind=kCustom, calls=%fused_computation.15 | custom fusion | flops 393216 | bytes 4719360 | tf_op jit(solution)/shard_map/scatter-add | solution.py:62
  52.3 9.8 %collective-permute-start.1 = (f32[16,32,64]{2,1,0:T(8,128)S(1)}, f32[16,32,64]{2,1,0:T(8,128)}, u32[]{:S(2)}, u32[]{:S(2)}) collective-permute-start(f32[16,32,64]{2,1,0:T(8,128)S(1)} %slice.71), channel_id=1, source_target_pairs={{0,255},{1,0},{2,1},{3,2},{4,3},{5,4},{6,5},{7,6},{8,7},{9,8},{10,... | collective-permute-start | bytes 393224 | tf_op jit(solution)/shard_map/ppermute | solution.py:29
  78.8 14.3 %fusion.81 = f32[64,32,64]{2,1,0:T(8,128)S(1)} fusion(f32[64,6,32,64]{3,2,1,0:T(8,128)} %bitcast.120, f32[64,7,64,64]{3,2,1,0:T(8,128)} %param.8), kind=kOutput, calls=%fused_computation.81 | convolution fusion | flops 603979776 | bytes 19398656 | tf_op jit(solution)/shard_map/nkab,nkrb->nra/dot_general | solution.py:35
  93.1 6.1 multiply_reduce_fusion.4
  99.2 83.5 %all-reduce = (f32[32]{0:T(128)S(1)}, f32[32]{0:T(128)S(1)}) all-reduce(f32[32]{0:T(128)S(1)} %get-tuple-element.3, f32[32]{0:T(128)S(1)} %get-tuple-element.2), channel_id=1, replica_groups=mesh['dom'=256] {'dom'}, use_global_device_ids=true, to_apply=%region_3.0 | all-reduce | flops 64 | bytes 512 | tf_op jit(solution)/shard_map/psum | solution.py:43
  190.9 9.4 %fusion.75 = f32[64,32,64]{2,1,0:T(8,128)S(1)} fusion(f32[64,3,32,64]{3,2,1,0:T(8,128)} %bitcast.127, f32[64,4,64,64]{3,2,1,0:T(8,128)} %param.10), kind=kOutput, calls=%fused_computation.79 | convolution fusion | flops 301989888 | bytes 9961472 | tf_op jit(solution)/shard_map/nkab,nkrb->nra/dot_general | solution.py:35
  205.3 7.7 %fusion.10 = f32[64,32,3,64]{3,1,2,0:T(8,128)} fusion(f32[64,4,64,64]{3,2,1,0:T(8,128)} %param.10, f32[64,32,64]{2,1,0:T(8,128)S(1)} %fusion.51), kind=kOutput, calls=%fused_computation.31 | convolution fusion | flops 301989888 | bytes 8388608 | tf_op jit(solution)/shard_map/nkab,nra->nkrb/dot_general | solution.py:61
  213.1 17.3 %scatter_fusion.2 = f32[80,32,64]{2,1,0:T(8,128)S(1)} fusion(f32[80,32,64]{2,1,0:T(8,128)S(1)} %broadcast.58.clone.1, s32[192]{0:T(256)S(1)} %reshape.199, f32[192,32,64]{2,1,0:T(8,128)} %bitcast.124), kind=kCustom, calls=%fused_computation.17 | custom fusion | flops 393216 | bytes 4719360 | tf_op jit(solution)/shard_map/scatter-add | solution.py:62
  230.4 9.0 %collective-permute-start.5 = (f32[16,32,64]{2,1,0:T(8,128)S(1)}, f32[16,32,64]{2,1,0:T(8,128)}, u32[]{:S(2)}, u32[]{:S(2)}) collective-permute-start(f32[16,32,64]{2,1,0:T(8,128)S(1)} %slice.73), channel_id=1, source_target_pairs={{0,255},{1,0},{2,1},{3,2},{4,3},{5,4},{6,5},{7,6},{8,7},{9,8},{10,... | collective-permute-start | bytes 393224 | tf_op jit(solution)/shard_map/ppermute | solution.py:29
  248.5 76.4 %psum.44 = f32[32]{0:T(128)S(1)} all-reduce(f32[32]{0:T(128)S(1)} %multiply_reduce_fusion.3), channel_id=1, replica_groups=mesh['dom'=256] {'dom'}, use_global_device_ids=true, to_apply=%region_9.0 | all-reduce | flops 32 | bytes 256 | tf_op jit(solution)/shard_map/psum | solution.py:43
  338.9 14.3 %fusion.84 = f32[64,32,64]{2,1,0:T(8,128)S(1)} fusion(f32[64,6,32,64]{3,2,1,0:T(8,128)} %bitcast.121, f32[64,7,64,64]{3,2,1,0:T(8,128)} %param.8), kind=kOutput, calls=%fused_computation.82 | convolution fusion | flops 603979776 | bytes 19398656 | tf_op jit(solution)/shard_map/nkab,nkrb->nra/dot_general | solution.py:35
  353.2 6.1 multiply_reduce_fusion.2
  359.3 83.5 %psum.45 = f32[32]{0:T(128)S(1)} all-reduce(f32[32]{0:T(128)S(1)} %get-tuple-element.9), channel_id=1, replica_groups=mesh['dom'=256] {'dom'}, use_global_device_ids=true, to_apply=%region_11.0 | all-reduce | flops 32 | bytes 256 | tf_op jit(solution)/shard_map/psum | solution.py:82
  454.6 9.4 %fusion.78 = f32[64,32,64]{2,1,0:T(8,128)S(1)} fusion(f32[64,3,32,64]{3,2,1,0:T(8,128)} %bitcast.125, f32[64,4,64,64]{3,2,1,0:T(8,128)} %param.10), kind=kOutput, calls=%fused_computation.80 | convolution fusion | flops 301989888 | bytes 9961472 | tf_op jit(solution)/shard_map/nkab,nkrb->nra/dot_general | solution.py:35
  469.0 7.7 %fusion.6 = f32[64,32,3,64]{3,1,2,0:T(8,128)} fusion(f32[64,4,64,64]{3,2,1,0:T(8,128)} %param.10, f32[64,32,64]{2,1,0:T(8,128)S(1)} %fusion.57), kind=kOutput, calls=%fused_computation.27 | convolution fusion | flops 301989888 | bytes 8388608 | tf_op jit(solution)/shard_map/nkab,nra->nkrb/dot_general | solution.py:61
  477.9 25.8 %scatter_fusion.4 = f32[80,32,64]{2,1,0:T(8,128)} fusion(f32[80,32,64]{2,1,0:T(8,128)} %broadcast.58, s32[192]{0:T(256)S(1)} %reshape.199, f32[192,32,64]{2,1,0:T(8,128)} %bitcast.122), kind=kCustom, calls=%fused_computation.19 | custom fusion | flops 393216 | bytes 4719360 | tf_op jit(solution)/shard_map/scatter-add | solution.py:62
  504.7 9.2 %collective-permute-start.9 = (f32[16,32,64]{2,1,0:T(8,128)S(1)}, f32[16,32,64]{2,1,0:T(8,128)}, u32[]{:S(2)}, u32[]{:S(2)}) collective-permute-start(f32[16,32,64]{2,1,0:T(8,128)S(1)} %slice.75), channel_id=1, source_target_pairs={{0,255},{1,0},{2,1},{3,2},{4,3},{5,4},{6,5},{7,6},{8,7},{9,8},{10,... | collective-permute-start | bytes 393224 | tf_op jit(solution)/shard_map/ppermute | solution.py:29
  513.9 5.1 fusion.60
  523.2 76.1 %psum.46 = f32[32]{0:T(128)S(1)} all-reduce(f32[32]{0:T(128)S(1)} %multiply_reduce_fusion.1), channel_id=1, replica_groups=mesh['dom'=256] {'dom'}, use_global_device_ids=true, to_apply=%region_15.0 | all-reduce | flops 32 | bytes 256 | tf_op jit(solution)/shard_map/psum | solution.py:43
  613.2 14.3 %fusion.87 = f32[64,32,64]{2,1,0:T(8,128)S(1)} fusion(f32[64,6,32,64]{3,2,1,0:T(8,128)} %bitcast.119, f32[64,7,64,64]{3,2,1,0:T(8,128)} %param.8), kind=kOutput, calls=%fused_computation.83 | convolution fusion | flops 603979776 | bytes 19398656 | tf_op jit(solution)/shard_map/nkab,nkrb->nra/dot_general | solution.py:35
  627.5 6.3 multiply_reduce_fusion
  633.8 83.5 %psum.47 = f32[32]{0:T(128)S(1)} all-reduce(f32[32]{0:T(128)S(1)} %get-tuple-element.11), channel_id=1, replica_groups=mesh['dom'=256] {'dom'}, use_global_device_ids=true, to_apply=%region_17.0 | all-reduce | flops 32 | bytes 256 | tf_op jit(solution)/shard_map/psum | solution.py:82
  (108 shorter events, 111.0 us)
Async XLA Ops:
  3.1 6.0 collective-permute-start
  13.0 9.5 %copy-start.8 = (f32[64,32,64]{2,1,0:T(8,128)S(1)}, f32[64,32,64]{2,1,0:T(8,128)}, u32[]{:S(2)}) copy-start(f32[64,32,64]{2,1,0:T(8,128)} %param.7) | copy-start | bytes 1572868
  52.3 17.2 %copy-start.12 = (s32[64,6]{0,1:T(8,128)S(1)}, s32[64,6]{0,1:T(8,128)}, u32[]{:S(2)}) copy-start(s32[64,6]{0,1:T(8,128)} %param.9) | copy-start | bytes 4612
  52.3 13.4 %collective-permute-start.1 = (f32[16,32,64]{2,1,0:T(8,128)S(1)}, f32[16,32,64]{2,1,0:T(8,128)}, u32[]{:S(2)}, u32[]{:S(2)}) collective-permute-start(f32[16,32,64]{2,1,0:T(8,128)S(1)} %slice.71), channel_id=1, source_target_pairs={{0,255},{1,0},{2,1},{3,2},{4,3},{5,4},{6,5},{7,6},{8,7},{9,8},{10,... | collective-permute-start | bytes 393224 | tf_op jit(solution)/shard_map/ppermute | solution.py:29
  68.2 3.4 collective-permute-start.2
  68.9 5.9 collective-permute-start.3
  78.8 14.3 %copy-start.9 = (f32[64,32,64]{2,1,0:T(8,128)S(1)}, f32[64,32,64]{2,1,0:T(8,128)}, u32[]{:S(2)}) copy-start(f32[64,32,64]{2,1,0:T(8,128)} %param.7) | copy-start | bytes 1572868
  184.2 62.8 %copy-start.5 = (f32[64,32,64]{2,1,0:T(8,128)}, f32[64,32,64]{2,1,0:T(8,128)S(1)}, u32[]{:S(2)}) copy-start(f32[64,32,64]{2,1,0:T(8,128)S(1)} %multiply_subtract_fusion.2) | copy-start | bytes 1572868
  184.8 3.4 collective-permute-start.4
  205.3 7.7 %copy-start.11 = (f32[64,32,64]{2,1,0:T(8,128)}, f32[64,32,64]{2,1,0:T(8,128)S(1)}, u32[]{:S(2)}) copy-start(f32[64,32,64]{2,1,0:T(8,128)S(1)} %fusion.51) | copy-start | bytes 1572868
  230.4 13.9 %collective-permute-start.5 = (f32[16,32,64]{2,1,0:T(8,128)S(1)}, f32[16,32,64]{2,1,0:T(8,128)}, u32[]{:S(2)}, u32[]{:S(2)}) collective-permute-start(f32[16,32,64]{2,1,0:T(8,128)S(1)} %slice.73), channel_id=1, source_target_pairs={{0,255},{1,0},{2,1},{3,2},{4,3},{5,4},{6,5},{7,6},{8,7},{9,8},{10,... | collective-permute-start | bytes 393224 | tf_op jit(solution)/shard_map/ppermute | solution.py:29
  326.4 4.6 copy-start
  327.5 3.4 collective-permute-start.6
  327.6 6.0 collective-permute-start.7
  338.9 14.3 %copy-start.1 = (f32[64,32,64]{2,1,0:T(8,128)S(1)}, f32[64,32,64]{2,1,0:T(8,128)}, u32[]{:S(2)}) copy-start(f32[64,32,64]{2,1,0:T(8,128)} %copy-done) | copy-start | bytes 1572868
  444.6 77.2 %copy-start.3 = (f32[64,32,64]{2,1,0:T(8,128)}, f32[64,32,64]{2,1,0:T(8,128)S(1)}, u32[]{:S(2)}) copy-start(f32[64,32,64]{2,1,0:T(8,128)S(1)} %multiply_subtract_fusion.1) | copy-start | bytes 1572868
  445.8 3.8 collective-permute-start.8
  469.0 7.7 %copy-start.10 = (f32[64,32,64]{2,1,0:T(8,128)}, f32[64,32,64]{2,1,0:T(8,128)S(1)}, u32[]{:S(2)}) copy-start(f32[64,32,64]{2,1,0:T(8,128)S(1)} %fusion.57) | copy-start | bytes 1572868
  504.7 14.4 %collective-permute-start.9 = (f32[16,32,64]{2,1,0:T(8,128)S(1)}, f32[16,32,64]{2,1,0:T(8,128)}, u32[]{:S(2)}, u32[]{:S(2)}) collective-permute-start(f32[16,32,64]{2,1,0:T(8,128)S(1)} %slice.75), channel_id=1, source_target_pairs={{0,255},{1,0},{2,1},{3,2},{4,3},{5,4},{6,5},{7,6},{8,7},{9,8},{10,... | collective-permute-start | bytes 393224 | tf_op jit(solution)/shard_map/ppermute | solution.py:29
  602.0 3.4 collective-permute-start.10
  602.1 5.9 collective-permute-start.11
  613.2 14.3 %copy-start.7 = (f32[64,32,64]{2,1,0:T(8,128)S(1)}, f32[64,32,64]{2,1,0:T(8,128)}, u32[]{:S(2)}) copy-start(f32[64,32,64]{2,1,0:T(8,128)} %copy-done.6) | copy-start | bytes 1572868
  627.5 89.8 %copy-start.2 = (f32[64,32,64]{2,1,0:T(8,128)S(1)}, f32[64,32,64]{2,1,0:T(8,128)}, u32[]{:S(2)}) copy-start(f32[64,32,64]{2,1,0:T(8,128)} %copy-done) | copy-start | bytes 1572868
  627.5 89.8 %copy-start.4 = (f32[64,32,64]{2,1,0:T(8,128)S(1)}, f32[64,32,64]{2,1,0:T(8,128)}, u32[]{:S(2)}) copy-start(f32[64,32,64]{2,1,0:T(8,128)} %copy-done.3) | copy-start | bytes 1572868
  (1 other events, 4.6 us)
where the time goes:
time: 732 us; the launch traced here: 721 us
  blocking collectives  403 us (55%)
  matrix products  141 us (19%)
  other arithmetic  88 us (12%)
  starting transfers between devices  34.2 us (5%)
  local copies, waits for them, and re-layouts  31.4 us (4%)
  waiting for transfers between devices  22.3 us (3%)
    psum x3, blocking collectives, residual_norm(): return lax.psum(inner_product(residual, precond), 'dom')  236 us
    psum x2, blocking collectives, body(): alpha = rz_now / lax.psum(inner_product(direction, image), 'dom')  167 us
    dot_general x6, matrix products, block_product(): jnp.einsum('nkab,nkrb->nra', off_blocks, nearby, precision=HIGH)  71.2 us
    scatter-add x3, other arithmetic, precondition(): jax.ops.segment_sum(partial_terms.reshape(-1, values.shape[1], values.sha...  60.3 us
    dot_general x6, matrix products, block_product(): jnp.einsum('nab,nrb->nra', diag_blocks, own_field, precision=HIGH)  33.4 us
    ppermute x6, starting transfers between devices, shifted(): return lax.ppermute(value, axis, pairs)  31 us
    dot_general x3, matrix products, precondition(): jnp.einsum('nkab,nra->nkrb', g_offdiag, values, precision=HIGH)  22.6 us
    gather x6, local copies, waits for them, and re-layouts, block_product(): nearby = extended[columns]  20.4 us
  transfers between devices with their start and end apart: 12, of which 9 were waited for; matrix products, arithmetic and copies ran while one was open for 2% of the time, Pallas kernels for 0%

commit v1 on v0

v1 whole, which is shorter than its diff:
```python
import jax
import jax.numpy as jnp
from jax import lax
from jax.experimental import pallas as pl
from jax.experimental.pallas import tpu as pltpu
from jax.sharding import PartitionSpec as P

ROWS = 64
FACE = 16
LAYERS = 4
RHS = 32
DOFS = 64
MESH = pl.DeviceIdType.MESH
NT = (((1,), (1,)), ((), ()))
F32 = jnp.float32
BF16 = jnp.bfloat16
G_CHUNK = 16
A_CHUNK = 8
A_SLOTS = 4
GROUPS = ((1, 16), (16, 16))


def loop(lo, hi, fn, unroll=None):
    def step(i, carry):
        fn(i)
        return carry

    lax.fori_loop(lo, hi, step, 0, unroll=(hi - lo) if unroll is None else unroll)


def kernel(rhs_hbm, a_hbm, g_hbm, cols, send_up, send_down, x_hbm, r_hbm,
           rhs_in, a_in, g_in, a_w, g_w, gz_w, packed_w, packed_y, packed_m,
           low_w, high_y, low_m, high_m, y_loc, y_far,
           r0, u0, w0, m0, n0, u1, w1, m1, n1, x_out, r_out,
           gz_send, gz_recv, halo_send, halo_recv, dot_send, dot_recv,
           place, inverse, near, low_at, high_at, inverse_vec,
           in_sem, a_sem, out_sem, tab_sem, gz_ssem, gz_rsem, halo_ssem, halo_rsem, dot_ssem, dot_rsem):
    count = lax.axis_size("dom")
    me = lax.axis_index("dom")
    above = lax.rem(me + 1, count)
    below = lax.rem(me + count - 1, count)

    def partner(stride, size, step):
        mine = lax.rem(me // stride, size)
        return me + (lax.rem(mine + step, size) - mine) * stride

    def rhs_copy():
        return pltpu.make_async_copy(rhs_hbm, rhs_in, in_sem.at[0])

    def g_copy(c):
        part = pl.ds(c * G_CHUNK, G_CHUNK)
        return pltpu.make_async_copy(g_hbm.at[part], g_in.at[part], in_sem.at[1 + c])

    def a_copy(c):
        return pltpu.make_async_copy(a_hbm.at[pl.ds(c * A_CHUNK, A_CHUNK)], a_in.at[c % A_SLOTS], a_sem.at[c % A_SLOTS])

    rhs_copy().start()
    for c in range(ROWS // G_CHUNK):
        g_copy(c).start()
    for c in range(A_SLOTS):
        a_copy(c).start()

    barrier = pltpu.get_barrier_semaphore()
    greeted = 2
    for device in (above, below):
        pl.semaphore_signal(barrier, inc=1, device_id=(device,), device_id_type=MESH)
    for stride, size in GROUPS:
        for step in range(1, size):
            pl.semaphore_signal(barrier, inc=1, device_id=(partner(stride, size, step),), device_id_type=MESH)
            greeted += 1

    def first_layer(h):
        place[h] = send_down[0, h]

    loop(0, FACE, first_layer)

    def next_layer(e):
        place[e + FACE] = cols[5, place[e]]

    loop(0, ROWS - FACE, next_layer, 1)
    tab_lane = lax.broadcasted_iota(jnp.int32, (8, 128), 1)
    vec = lax.fori_loop(0, ROWS, lambda e, v: jnp.where(tab_lane == place[e], e, v),
                        jnp.zeros((8, 128), jnp.int32), unroll=8)
    inverse_vec[...] = vec
    tab = pltpu.make_async_copy(inverse_vec, inverse, tab_sem)
    tab.start()
    tab.wait()

    def neighbours(e):
        row = place[e]
        for k in range(4):
            near[e * 4 + k] = inverse[0, cols[k, row]]

    loop(0, ROWS, neighbours, 4)

    def crossings(h):
        low_at[h] = jnp.clip(cols[4, place[h]] - ROWS, 0, FACE - 1)
        high_at[h] = jnp.clip(cols[5, place[3 * FACE + h]] - (ROWS + FACE), 0, FACE - 1)

    loop(0, FACE, crossings, 4)

    left = lax.broadcasted_iota(jnp.int32, (RHS, 128), 1) < DOFS
    left2 = lax.broadcasted_iota(jnp.int32, (2 * RHS, 128), 1) < DOFS

    def twice(v):
        return jnp.concatenate([v, v], axis=1)

    def split(ref, e, v):
        hi = v.astype(BF16)
        ref[e, 0:RHS] = hi
        ref[e, RHS:2 * RHS] = (v - hi.astype(F32)).astype(BF16)

    def split_block(v):
        hi = v.astype(BF16)
        lo = (v - hi.astype(F32)).astype(BF16)
        return jnp.concatenate([hi, lo], axis=1)

    def times(fields, weights):
        out = lax.dot_general(jnp.concatenate(fields, axis=1), jnp.concatenate(weights, axis=1), NT,
                              preferred_element_type=F32)
        return out[:RHS] + out[RHS:]

    def times_transposed(fields, weights):
        pair = [jnp.where(left2, fields[0], fields[1]), jnp.where(left2, fields[2], fields[3])]
        out = jnp.dot(jnp.concatenate(pair, axis=1), jnp.concatenate(weights, axis=0), preferred_element_type=F32)
        out = out[:RHS] + out[RHS:]
        return out + pltpu.roll(out, DOFS, 1)

    def convert_g(c):
        g_copy(c).wait()

        def one(b):
            i = c * G_CHUNK + b // 4
            k = b % 4
            g_w[i * 4 + k] = split_block(g_in[i, k])

        loop(0, G_CHUNK * 4, one, 16)

    def convert_a(c):
        a_copy(c).wait()
        slot = c % A_SLOTS

        def one(i):
            for k in range(7):
                a_w[(c * A_CHUNK + i) * 7 + k] = split_block(a_in[slot, i, k])

        loop(0, A_CHUNK, one, 2)
        if c + A_SLOTS < ROWS // A_CHUNK:
            a_copy(c + A_SLOTS).start()

    def halo_copy(slot):
        return pltpu.make_async_remote_copy(
            src_ref=halo_send.at[slot], dst_ref=halo_recv.at[slot], send_sem=halo_ssem.at[slot],
            recv_sem=halo_rsem.at[slot], device_id=(above if slot % 2 == 0 else below,), device_id_type=MESH)

    def send_top(slot, field):
        def one(j):
            halo_send[slot, j] = jnp.where(left, field[inverse[0, send_up[0, 2 * j]]],
                                           field[inverse[0, send_up[0, 2 * j + 1]]])

        loop(0, FACE // 2, one)
        halo_copy(slot).start()

    def send_bottom(slot, field):
        def one(j):
            halo_send[slot, j] = jnp.where(left, field[2 * j], field[2 * j + 1])

        loop(0, FACE // 2, one)
        halo_copy(slot).start()

    def halves(v):
        turned = pltpu.roll(v, DOFS, 1)
        return jnp.where(left, v, turned), jnp.where(left, turned, v)

    def unpack_split(slot, ref):
        def one(j):
            first, second = halves(halo_recv[slot, j])
            split(ref, 2 * j, first)
            split(ref, 2 * j + 1, second)

        loop(0, FACE // 2, one)

    def row_y(e, below_block):
        row = place[e] * 4
        return times([packed_w[e], packed_w[near[e * 4]], packed_w[near[e * 4 + 2]], below_block],
                     [g_w[row], g_w[row + 1], g_w[row + 2], g_w[row + 3]])

    def row_u(e, above_block, above_weight):
        ex = near[e * 4 + 1]
        ey = near[e * 4 + 3]
        return times_transposed(
            [packed_y[e], packed_y[ex], packed_y[ey], above_block],
            [g_w[place[e] * 4], g_w[place[ex] * 4 + 1], g_w[place[ey] * 4 + 2], above_weight])

    def row_a(e, below_block, above_block):
        row = place[e] * 7
        return twice(times(
            [packed_m[e]] + [packed_m[near[e * 4 + k]] for k in range(4)] + [below_block, above_block],
            [a_w[row + k] for k in range(7)]))

    def product(number, field, out_m, out_n, beside_first, beside_second):
        base = number * 4
        send_top(base, field)

        def bottom(h):
            row = place[h] * 4
            v = times([packed_w[h], packed_w[near[h * 4]], packed_w[near[h * 4 + 2]]],
                      [g_w[row], g_w[row + 1], g_w[row + 2]])
            y_loc[h] = twice(v)

        loop(0, FACE, bottom)
        send_bottom(base + 1, y_loc)
        beside_first()

        def inner_y(e):
            split(packed_y, e, twice(row_y(e, packed_w[e - FACE])))

        loop(FACE, ROWS, inner_y)

        def put_u(e, v):
            out_m[e] = v
            split(packed_m, e, v)

        def inner_u(e):
            put_u(e, row_u(e, packed_y[e + FACE], g_w[place[e + FACE] * 4 + 3]))

        loop(FACE, 3 * FACE, inner_u)

        halo_copy(base).wait_recv()
        halo_copy(base + 1).wait_recv()
        unpack_split(base, low_w)

        def edge_y(j):
            pair = halves(halo_recv[base + 1, j])
            for s in range(2):
                y_far[2 * j + s] = pair[s]

        loop(0, FACE // 2, edge_y)

        def close_y(h):
            extra = times([low_w[low_at[h]]], [g_w[place[h] * 4 + 3]])
            split(packed_y, h, y_loc[h] + twice(extra))
            t = high_at[h]
            more = times([packed_w[3 * FACE + h]], [gz_w[t]])
            split(high_y, h, y_far[t] + twice(more))

        loop(0, FACE, close_y)

        def outer_u(h):
            put_u(h, row_u(h, packed_y[h + FACE], g_w[place[h + FACE] * 4 + 3]))
            e = 3 * FACE + h
            put_u(e, row_u(e, high_y[h], gz_w[high_at[h]]))

        loop(0, FACE, outer_u)
        send_bottom(base + 3, out_m)
        send_top(base + 2, out_m)
        beside_second()

        def inner_a(e):
            out_n[e] = row_a(e, packed_m[e - FACE], packed_m[e + FACE])

        loop(FACE, 3 * FACE, inner_a)
        halo_copy(base + 2).wait_recv()
        halo_copy(base + 3).wait_recv()
        unpack_split(base + 2, low_m)
        unpack_split(base + 3, high_m)

        def outer_a(h):
            out_n[h] = row_a(h, low_m[low_at[h]], packed_m[h + FACE])
            e = 3 * FACE + h
            out_n[e] = row_a(e, packed_m[e - FACE], high_m[high_at[h]])

        loop(0, FACE, outer_a)


    dot_lane = lax.broadcasted_iota(jnp.int32, (8, 128), 1)

    def dot_copies(number, stage):
        stride, size = GROUPS[stage]
        return [pltpu.make_async_remote_copy(
            src_ref=dot_send.at[number, stage], dst_ref=dot_recv.at[number, stage, step - 1],
            send_sem=dot_ssem.at[number, stage], recv_sem=dot_rsem.at[number, stage],
            device_id=(partner(stride, size, step),), device_id_type=MESH) for step in range(1, size)]

    def dot_start(number, stage, value):
        dot_send[number, stage] = value
        for c in dot_copies(number, stage):
            c.start()

    def dot_finish(number, stage):
        slots = dot_recv.at[number, stage]
        pltpu.make_async_copy(slots, slots, dot_rsem.at[number, stage]).wait()
        return dot_send[number, stage] + jnp.sum(dot_recv[number, stage], axis=0)

    def dot_pack(first, second):
        first = jnp.sum(first, axis=1, keepdims=True)
        second = jnp.sum(second, axis=1, keepdims=True)
        out = jnp.zeros((8, 128), F32)
        for g in range(4):
            out = jnp.where(dot_lane == 2 * g, first[8 * g:8 * g + 8], out)
            out = jnp.where(dot_lane == 2 * g + 1, second[8 * g:8 * g + 8], out)
        return out

    def dot_unpack(v):
        first = jnp.concatenate([v[:, 2 * g:2 * g + 1] for g in range(4)], axis=0)
        second = jnp.concatenate([v[:, 2 * g + 1:2 * g + 2] for g in range(4)], axis=0)
        return first, second

    zero = jnp.zeros((RHS, 128), F32)

    rhs_copy().wait()

    def load_rhs(e):
        v = twice(rhs_in[place[e]])
        r0[e] = v
        split(packed_w, e, v)

    loop(0, ROWS, load_rhs, 16)
    for c in range(ROWS // G_CHUNK):
        convert_g(c)
    pl.semaphore_wait(barrier, greeted)

    def gz_copy():
        return pltpu.make_async_remote_copy(src_ref=gz_send, dst_ref=gz_recv, send_sem=gz_ssem, recv_sem=gz_rsem,
                                            device_id=(below,), device_id_type=MESH)

    def fill_gz(j):
        gz_send[j] = jnp.concatenate([g_in[place[2 * j], 3], g_in[place[2 * j + 1], 3]], axis=1)

    def first_side():
        loop(0, FACE // 2, fill_gz)
        gz_copy().start()
        for c in range(ROWS // A_CHUNK - 2):
            convert_a(c)
        gz_copy().wait_recv()

        def one(j):
            v = gz_recv[j]
            gz_w[2 * j] = split_block(v[:, :DOFS])
            gz_w[2 * j + 1] = split_block(v[:, DOFS:])

        loop(0, FACE // 2, one)

    def second_side():
        for c in range(ROWS // A_CHUNK - 2, ROWS // A_CHUNK):
            convert_a(c)

    product(0, r0, u0, w0, first_side, second_side)

    def dots0(e, carry):
        split(packed_w, e, w0[e])
        return carry[0] + r0[e] * u0[e], carry[1] + w0[e] * u0[e]

    value = dot_pack(*lax.fori_loop(0, ROWS, dots0, (zero, zero), unroll=16))
    dot_start(0, 0, value)

    def middle(number):
        def run():
            dot_start(number, 1, dot_finish(number, 0))
        return run

    def nothing():
        pass

    product(1, w0, m0, n0, nothing, middle(0))
    gam0, del0 = dot_unpack(dot_finish(0, 1))
    alpha0 = gam0 / del0
    al0 = jnp.broadcast_to(alpha0, (RHS, 128))

    def update0(e, carry):
        u = u0[e] - al0 * m0[e]
        w = w0[e] - al0 * n0[e]
        r = r0[e] - al0 * w0[e]
        u1[e] = u
        w1[e] = w
        split(packed_w, e, w)
        return carry[0] + r * u, carry[1] + w * u

    value = dot_pack(*lax.fori_loop(0, ROWS, update0, (zero, zero), unroll=16))
    dot_start(1, 0, value)

    product(2, w1, m1, n1, nothing, middle(1))
    gam1, del1 = dot_unpack(dot_finish(1, 1))
    beta1 = gam1 / gam0
    alpha1 = gam1 / (del1 - beta1 * gam1 / alpha0)
    al1 = jnp.broadcast_to(alpha1, (RHS, 128))
    ab1 = jnp.broadcast_to(alpha1 * beta1, (RHS, 128))
    be1 = jnp.broadcast_to(beta1, (RHS, 128))
    k0 = jnp.broadcast_to(alpha0 + alpha1 * beta1, (RHS, 128))

    def update1(e, carry):
        u = u1[e] - (al1 * m1[e] + ab1 * m0[e])
        w = w1[e] - (al1 * n1[e] + ab1 * n0[e])
        r = r0[e] - (k0 * w0[e] + al1 * w1[e])
        m1[e] = u
        n1[e] = w
        return carry[0] + r * u, carry[1] + w * u

    value = dot_pack(*lax.fori_loop(0, ROWS, update1, (zero, zero), unroll=16))
    dot_start(2, 0, value)

    def prepare(e):
        u, w = u0[e], w0[e]
        v, q = u1[e], w1[e]
        m0[e] = k0 * u + al1 * v
        u0[e] = v + be1 * u
        n0[e] = r0[e] - (k0 * w + al1 * q)
        w0[e] = q + be1 * w

    loop(0, ROWS, prepare, 16)
    dot_start(2, 1, dot_finish(2, 0))
    gam2, del2 = dot_unpack(dot_finish(2, 1))
    beta2 = gam2 / gam1
    alpha2 = gam2 / (del2 - beta2 * gam2 / alpha1)
    al2 = jnp.broadcast_to(alpha2, (RHS, 128))
    ab2 = jnp.broadcast_to(alpha2 * beta2, (RHS, 128))

    def finish_x(i):
        e = inverse[0, i]
        x_out[i] = (m0[e] + (al2 * m1[e] + ab2 * u0[e]))[:, :DOFS]

    def finish_r(i):
        e = inverse[0, i]
        r_out[i] = (n0[e] - (al2 * n1[e] + ab2 * w0[e]))[:, :DOFS]

    loop(0, ROWS, finish_x, 16)
    x_copy = pltpu.make_async_copy(x_out, x_hbm, out_sem.at[0])
    x_copy.start()
    loop(0, ROWS, finish_r, 16)
    r_copy = pltpu.make_async_copy(r_out, r_hbm, out_sem.at[1])
    r_copy.start()
    x_copy.wait()
    r_copy.wait()

    gz_copy().wait_send()
    for slot in range(12):
        halo_copy(slot).wait_send()
    for number in range(3):
        for stage in range(2):
            slots = dot_recv.at[number, stage]
            pltpu.make_async_copy(slots, slots, dot_ssem.at[number, stage]).wait()


def body(right_side, a_blocks, a_cols, g_blocks, g_cols, send_up, send_down):
    field = pltpu.VMEM((ROWS, RHS, 128), F32)
    packed = pltpu.VMEM((ROWS, 2 * RHS, 128), BF16)
    face = pltpu.VMEM((FACE, 2 * RHS, 128), BF16)
    hbm = pl.BlockSpec(memory_space=pl.ANY)
    smem = pl.BlockSpec(memory_space=pltpu.SMEM)
    dma = pltpu.SemaphoreType.DMA
    out = jax.ShapeDtypeStruct((ROWS, RHS, DOFS), F32)
    return pl.pallas_call(
        kernel,
        out_shape=(out, out),
        in_specs=[hbm, hbm, hbm, smem, smem, smem],
        out_specs=(hbm, hbm),
        scratch_shapes=[
            pltpu.VMEM((ROWS, RHS, DOFS), F32),
            pltpu.VMEM((A_SLOTS, A_CHUNK, 7, DOFS, DOFS), F32),
            pltpu.VMEM((ROWS, 4, DOFS, DOFS), F32),
            pltpu.VMEM((ROWS * 7, DOFS, 128), BF16),
            pltpu.VMEM((ROWS * 4, DOFS, 128), BF16),
            pltpu.VMEM((FACE, DOFS, 128), BF16),
            packed, packed, packed,
            face, face, face, face,
            pltpu.VMEM((FACE, RHS, 128), F32),
            pltpu.VMEM((FACE, RHS, 128), F32),
            field, field, field, field, field, field, field, field, field,
            pltpu.VMEM((ROWS, RHS, DOFS), F32),
            pltpu.VMEM((ROWS, RHS, DOFS), F32),
            pltpu.VMEM((FACE // 2, DOFS, 128), F32),
            pltpu.VMEM((FACE // 2, DOFS, 128), F32),
            pltpu.VMEM((12, FACE // 2, RHS, 128), F32),
            pltpu.VMEM((12, FACE // 2, RHS, 128), F32),
            pltpu.VMEM((3, 2, 8, 128), F32),
            pltpu.VMEM((3, 2, 15, 8, 128), F32),
            pltpu.SMEM((ROWS,), jnp.int32),
            pltpu.SMEM((8, 128), jnp.int32),
            pltpu.SMEM((ROWS * 4,), jnp.int32),
            pltpu.SMEM((FACE,), jnp.int32),
            pltpu.SMEM((FACE,), jnp.int32),
            pltpu.VMEM((8, 128), jnp.int32),
            dma((5,)), dma((A_SLOTS,)), dma((2,)), dma, dma, dma,
            dma((12,)), dma((12,)), dma((3, 2)), dma((3, 2)),
        ],
        compiler_params=pltpu.CompilerParams(
            collective_id=0, has_side_effects=True, vmem_limit_bytes=60 * 2 ** 20),
    )(right_side, a_blocks, g_blocks, a_cols.T, send_up, send_down)


def solution(mesh):
    in_specs = (
        P("dom", None, None),
        P("dom", None, None, None),
        P("dom", None),
        P("dom", None, None, None),
        P("dom", None),
        P("dom", None),
        P("dom", None),
    )
    out_specs = (P("dom", None, None), P("dom", None, None))
    return jax.shard_map(body, mesh=mesh, in_specs=in_specs, out_specs=out_specs, check_vma=False)
```

time: 732 us -> 78.5 us (0.11); the launches traced: 721 us -> 78.3 us
  blocking collectives: 403 us -> 0 us
  matrix products: 141 us -> 0 us
  other arithmetic: 88 us -> 0 us
  Pallas kernels: 0 us -> 73.1 us
  starting transfers between devices: 34.2 us -> 0 us
  local copies, waits for them, and re-layouts: 31.4 us -> 4.52 us
  waiting for transfers between devices: 22.3 us -> 0 us
    psum x5 -> x0, blocking collectives: 403 us -> none  [the longest x3 236 us: residual_norm(): return lax.psum(inner_product(residual, precond), 'dom')]
    dot_general x18 -> x0, matrix products: 141 us -> none  [the longest x6 71.2 us: block_product(): jnp.einsum('nkab,nkrb->nra', off_blocks, nearby, precision=HIGH)]
    pallas_call x0 -> x1, Pallas kernels: none -> 73.1 us  [body(): pl.pallas_call(kernel, out_shape=(out, out), in_specs=[hbm, hbm, hbm, sme...]
    scatter-add x6 -> x0, other arithmetic: 67.6 us -> none  [the longest x3 60.3 us: precondition(): jax.ops.segment_sum(partial_terms.reshape(-1, values.shape[1], values.sha...]
    ppermute x12 -> x0, starting transfers between devices: 34.2 us -> none  [the longest x6 31 us: shifted(): return lax.ppermute(value, axis, pairs)]
    gather x15 -> x0, local copies, waits for them, and re-layouts: 27.4 us -> none  [the longest x6 20.4 us: block_product(): nearby = extended[columns]]
    ppermute x12 -> x0, waiting for transfers between devices: 22.3 us -> none  [the longest x3 8.44 us: padded_2(): lax.ppermute(lax.slice_in_dim(block, 0, width, axis=dim), axis, backward)]
  transfers between devices with their start and end apart: 12 -> 0, of which waited for: 9 -> 0; matrix products, arithmetic and copies ran while one was open for 2% -> 0% of each run, Pallas kernels for 0% -> 0%
where the time goes in v1:
time: 78.5 us; the launch traced here: 78.3 us
  Pallas kernels  73.1 us (93%)
  local copies, waits for them, and re-layouts  4.52 us (6%)
    pallas_call x1, Pallas kernels, body(): pl.pallas_call(kernel, out_shape=(out, out), in_specs=[hbm, hbm, hbm, sme...  73.1 us
    unnamed x2, local copies, waits for them, and re-layouts  4.52 us

profile of v1, /device:TPU:1, one launch (start us, length us, event | category | flops | bytes accessed | tf_op | source)
XLA Modules:
  0.0 78.3 jit_solution(17509603046972835583)
XLA Ops:
  0.6 73.1 %shard_map.77 = (f32[64,32,64]{2,1,0:T(8,128)}, f32[64,32,64]{2,1,0:T(8,128)}) custom-call(f32[64,32,64]{2,1,0:T(8,128)} %rhs_hbm.1, f32[64,7,64,64]{3,2,1,0:T(8,128)} %a_hbm.1, f32[64,4,64,64]{3,2,1,0:T(8,128)} %g_hbm.1, s32[6,64]{1,0:T(8,128)} %bitcast.1, s32[1,16]{1,0:T(1,128)} %send_up.1, s32[1,16]{1,0:T(1,128)} %send_down.1), custom_call_target="tpu_custom_call" | custom-call | tf_op jit(solution)/shard_map/pallas_call | solution.py:452
  73.7 2.3 %copy.10 = f32[64,32,64]{2,1,0:T(8,128)} copy(f32[64,32,64]{2,1,0:T(8,128)} %get-tuple-element.4) | data formatting | bytes 1048576
  76.0 2.3 %copy.11 = f32[64,32,64]{2,1,0:T(8,128)} copy(f32[64,32,64]{2,1,0:T(8,128)} %get-tuple-element.5) | data formatting | bytes 1048576

commit v2 on v1

--- a/solution.py
+++ b/solution.py
@@ -1,3 +1,5 @@
+import itertools
+
 import jax
 import jax.numpy as jnp
 from jax import lax
@@ -17,7 +19,8 @@
 G_CHUNK = 16
 A_CHUNK = 8
 A_SLOTS = 4
-GROUPS = ((1, 16), (16, 16))
+GROUPS = (((1, 2), (2, 4), (64, 4)), ((8, 8),))
+FIRST_SLOT = (0, 31, 38)
 
 
 def loop(lo, hi, fn, unroll=None):
@@ -28,21 +31,29 @@
     lax.fori_loop(lo, hi, step, 0, unroll=(hi - lo) if unroll is None else unroll)
 
 
-def kernel(rhs_hbm, a_hbm, g_hbm, cols, send_up, send_down, x_hbm, r_hbm,
-           rhs_in, a_in, g_in, a_w, g_w, gz_w, packed_w, packed_y, packed_m,
-           low_w, high_y, low_m, high_m, y_loc, y_far,
-           r0, u0, w0, m0, n0, u1, w1, m1, n1, x_out, r_out,
-           gz_send, gz_recv, halo_send, halo_recv, dot_send, dot_recv,
-           place, inverse, near, low_at, high_at, inverse_vec,
-           in_sem, a_sem, out_sem, tab_sem, gz_ssem, gz_rsem, halo_ssem, halo_rsem, dot_ssem, dot_rsem):
+def kernel(rhs_hbm, a_hbm, g_hbm, cols, send_up, send_down, parts_hbm, alpha_hbm, alpha_beta_hbm,
+           rhs_in, a_in, g_in, a_w, g_w, gz_w, g0_w, packed_w, packed_y, packed_m,
+           low_w, high_y, low_m, high_m, low_t, high_t, y_loc, y_far, u_low, u_high,
+           r0, u0, w0, m0, n0, u1, w1, m1, n1, parts, coef,
+           gz_send, gz_recv, g0_send, g0_recv, halo_send, halo_recv, dot_send, dot_recv,
+           place, inverse, near, low_at, high_at, low_side, high_side, inverse_vec,
+           in_sem, a_sem, out_sem, tab_sem, gz_ssem, gz_rsem, g0_ssem, g0_rsem, halo_ssem, halo_rsem, dot_ssem, dot_rsem):
     count = lax.axis_size("dom")
     me = lax.axis_index("dom")
     above = lax.rem(me + 1, count)
     below = lax.rem(me + count - 1, count)
 
-    def partner(stride, size, step):
-        mine = lax.rem(me // stride, size)
-        return me + (lax.rem(mine + step, size) - mine) * stride
+    def partners(stage):
+        out = []
+        for steps in itertools.product(*[range(size) for _, size in GROUPS[stage]]):
+            device = me
+            for (stride, size), step in zip(GROUPS[stage], steps):
+                if step:
+                    mine = lax.rem(me // stride, size)
+                    device = device + (lax.rem(mine + step, size) - mine) * stride
+            if any(steps):
+                out.append(device)
+        return out
 
     def rhs_copy():
         return pltpu.make_async_copy(rhs_hbm, rhs_in, in_sem.at[0])
@@ -64,9 +75,9 @@
     greeted = 2
     for device in (above, below):
         pl.semaphore_signal(barrier, inc=1, device_id=(device,), device_id_type=MESH)
-    for stride, size in GROUPS:
-        for step in range(1, size):
-            pl.semaphore_signal(barrier, inc=1, device_id=(partner(stride, size, step),), device_id_type=MESH)
+    for stage in range(2):
+        for device in partners(stage):
+            pl.semaphore_signal(barrier, inc=1, device_id=(device,), device_id_type=MESH)
             greeted += 1
 
     def first_layer(h):
@@ -97,6 +108,10 @@
         low_at[h] = jnp.clip(cols[4, place[h]] - ROWS, 0, FACE - 1)
         high_at[h] = jnp.clip(cols[5, place[3 * FACE + h]] - (ROWS + FACE), 0, FACE - 1)
 
+        for s in range(2):
+            low_side[h * 2 + s] = jnp.clip(near[h * 4 + 1 + 2 * s], 0, FACE - 1)
+            high_side[h * 2 + s] = jnp.clip(near[(3 * FACE + h) * 4 + 1 + 2 * s] - 3 * FACE, 0, FACE - 1)
+
     loop(0, FACE, crossings, 4)
 
     left = lax.broadcasted_iota(jnp.int32, (RHS, 128), 1) < DOFS
@@ -121,20 +136,20 @@
         return out[:RHS] + out[RHS:]
 
     def times_transposed(fields, weights):
-        pair = [jnp.where(left2, fields[0], fields[1]), jnp.where(left2, fields[2], fields[3])]
+        pair = [jnp.where(left2, fields[i], fields[i + 1]) for i in range(0, len(fields) - 1, 2)]
+        if len(fields) % 2:
+            pair.append(fields[-1][:, :DOFS])
         out = jnp.dot(jnp.concatenate(pair, axis=1), jnp.concatenate(weights, axis=0), preferred_element_type=F32)
         out = out[:RHS] + out[RHS:]
         return out + pltpu.roll(out, DOFS, 1)
 
     def convert_g(c):
-        g_copy(c).wait()
-
         def one(b):
             i = c * G_CHUNK + b // 4
             k = b % 4
             g_w[i * 4 + k] = split_block(g_in[i, k])
 
-        loop(0, G_CHUNK * 4, one, 16)
+        loop(0, G_CHUNK * 4, one)
 
     def convert_a(c):
         a_copy(c).wait()
@@ -144,7 +159,7 @@
             for k in range(7):
                 a_w[(c * A_CHUNK + i) * 7 + k] = split_block(a_in[slot, i, k])
 
-        loop(0, A_CHUNK, one, 2)
+        loop(0, A_CHUNK, one)
         if c + A_SLOTS < ROWS // A_CHUNK:
             a_copy(c + A_SLOTS).start()
 
@@ -171,6 +186,12 @@
     def halves(v):
         turned = pltpu.roll(v, DOFS, 1)
         return jnp.where(left, v, turned), jnp.where(left, turned, v)
+
+    def unpack(slot, ref):
+        def one(j):
+            ref[2 * j], ref[2 * j + 1] = halves(halo_recv[slot, j])
+
+        loop(0, FACE // 2, one)
 
     def unpack_split(slot, ref):
         def one(j):
@@ -198,23 +219,20 @@
             [packed_m[e]] + [packed_m[near[e * 4 + k]] for k in range(4)] + [below_block, above_block],
             [a_w[row + k] for k in range(7)]))
 
-    def product(number, field, out_m, out_n, beside_first, beside_second):
-        base = number * 4
-        send_top(base, field)
-
-        def bottom(h):
-            row = place[h] * 4
-            v = times([packed_w[h], packed_w[near[h * 4]], packed_w[near[h * 4 + 2]]],
-                      [g_w[row], g_w[row + 1], g_w[row + 2]])
-            y_loc[h] = twice(v)
-
+    def bottom(h):
+        row = place[h] * 4
+        v = twice(times([packed_w[h], packed_w[near[h * 4]], packed_w[near[h * 4 + 2]]],
+                        [g_w[row], g_w[row + 1], g_w[row + 2]]))
+        y_loc[h] = v
+        split(packed_y, h, v)
+
+    def inner_y(e):
+        split(packed_y, e, twice(row_y(e, packed_w[e - FACE])))
+
+    def first_product(field, out_m, out_n, beside_first, beside_second):
         loop(0, FACE, bottom)
-        send_bottom(base + 1, y_loc)
+        send_bottom(1, y_loc)
         beside_first()
-
-        def inner_y(e):
-            split(packed_y, e, twice(row_y(e, packed_w[e - FACE])))
-
         loop(FACE, ROWS, inner_y)
 
         def put_u(e, v):
@@ -225,17 +243,10 @@
             put_u(e, row_u(e, packed_y[e + FACE], g_w[place[e + FACE] * 4 + 3]))
 
         loop(FACE, 3 * FACE, inner_u)
-
-        halo_copy(base).wait_recv()
-        halo_copy(base + 1).wait_recv()
-        unpack_split(base, low_w)
-
-        def edge_y(j):
-            pair = halves(halo_recv[base + 1, j])
-            for s in range(2):
-                y_far[2 * j + s] = pair[s]
-
-        loop(0, FACE // 2, edge_y)
+        halo_copy(0).wait_recv()
+        halo_copy(1).wait_recv()
+        unpack_split(0, low_w)
+        unpack(1, y_far)
 
         def close_y(h):
             extra = times([low_w[low_at[h]]], [g_w[place[h] * 4 + 3]])
@@ -252,18 +263,18 @@
             put_u(e, row_u(e, high_y[h], gz_w[high_at[h]]))
 
         loop(0, FACE, outer_u)
-        send_bottom(base + 3, out_m)
-        send_top(base + 2, out_m)
+        send_bottom(3, out_m)
+        send_top(2, out_m)
         beside_second()
 
         def inner_a(e):
             out_n[e] = row_a(e, packed_m[e - FACE], packed_m[e + FACE])
 
         loop(FACE, 3 * FACE, inner_a)
-        halo_copy(base + 2).wait_recv()
-        halo_copy(base + 3).wait_recv()
-        unpack_split(base + 2, low_m)
-        unpack_split(base + 3, high_m)
+        halo_copy(2).wait_recv()
+        halo_copy(3).wait_recv()
+        unpack_split(2, low_m)
+        unpack_split(3, high_m)
 
         def outer_a(h):
             out_n[h] = row_a(h, low_m[low_at[h]], packed_m[h + FACE])
@@ -272,25 +283,109 @@
 
         loop(0, FACE, outer_a)
 
+    def later_product(number, field, out_m, out_n, beside):
+        base = number * 4
+        send_top(base, field)
+        loop(0, FACE, bottom)
+        send_bottom(base + 1, y_loc)
+        loop(FACE, 2 * FACE, inner_y)
+        loop(3 * FACE, ROWS, inner_y)
+
+        def part_u(h):
+            out_m[h] = row_u(h, packed_y[h + FACE], g_w[place[h + FACE] * 4 + 3])
+            e = 3 * FACE + h
+            ex = near[e * 4 + 1]
+            ey = near[e * 4 + 3]
+            out_m[e] = times_transposed([packed_y[e], packed_y[ex], packed_y[ey]],
+                                        [g_w[place[e] * 4], g_w[place[ex] * 4 + 1], g_w[place[ey] * 4 + 2]])
+
+        loop(0, FACE, part_u)
+        send_bottom(base + 3, out_m)
+        send_top(base + 2, out_m)
+        loop(2 * FACE, 3 * FACE, inner_y)
+
+        def put_u(e, v):
+            out_m[e] = v
+            split(packed_m, e, v)
+
+        def inner_u(e):
+            put_u(e, row_u(e, packed_y[e + FACE], g_w[place[e + FACE] * 4 + 3]))
+
+        loop(FACE, 3 * FACE, inner_u)
+
+        def part_a(h):
+            for layer, k, other in ((1, 6, 2), (2, 5, 1)):
+                e = layer * FACE + h
+                row = place[e] * 7
+                out_n[e] = twice(times(
+                    [packed_m[e]] + [packed_m[near[e * 4 + i]] for i in range(4)] + [packed_m[other * FACE + h]],
+                    [a_w[row + i] for i in range(5)] + [a_w[row + k]]))
+
+        loop(0, FACE, part_a)
+        beside()
+        halo_copy(base).wait_recv()
+        halo_copy(base + 1).wait_recv()
+        unpack_split(base, low_w)
+        unpack(base + 1, y_far)
+
+        def close_y(h):
+            extra = twice(times([low_w[low_at[h]]], [g_w[place[h] * 4 + 3]]))
+            split(low_t, h, extra)
+            split(packed_y, h, y_loc[h] + extra)
+            t = high_at[h]
+            more = twice(times([packed_w[3 * FACE + h]], [gz_w[t]]))
+            split(high_t, h, more)
+            split(high_y, h, y_far[t] + more)
+
+        loop(0, FACE, close_y)
+        halo_copy(base + 2).wait_recv()
+        halo_copy(base + 3).wait_recv()
+        unpack(base + 2, u_low)
+        unpack(base + 3, u_high)
+
+        def close_u(h):
+            ex, ey = low_side[2 * h], low_side[2 * h + 1]
+            put_u(h, out_m[h] + times_transposed(
+                [low_t[h], low_t[ex], low_t[ey]],
+                [g_w[place[h] * 4], g_w[place[ex] * 4 + 1], g_w[place[ey] * 4 + 2]]))
+            e = 3 * FACE + h
+            put_u(e, out_m[e] + times_transposed([high_y[h]], [gz_w[high_at[h]]]))
+            split(low_m, h, u_low[low_at[h]] + times_transposed([packed_y[h]], [g_w[place[h] * 4 + 3]]))
+            hx, hy = high_side[2 * h], high_side[2 * h + 1]
+            split(high_m, h, u_high[high_at[h]] + times_transposed(
+                [high_t[h], high_t[hx], high_t[hy]],
+                [g0_w[high_at[h] * 3], g0_w[high_at[hx] * 3 + 1], g0_w[high_at[hy] * 3 + 2]]))
+
+        loop(0, FACE, close_u)
+
+        def close_a(h):
+            out_n[h] = row_a(h, low_m[h], packed_m[h + FACE])
+            e = 3 * FACE + h
+            out_n[e] = row_a(e, packed_m[e - FACE], high_m[h])
+            for layer, k, other in ((1, 5, 0), (2, 6, 3)):
+                e = layer * FACE + h
+                out_n[e] = out_n[e] + twice(times([packed_m[other * FACE + h]], [a_w[place[e] * 7 + k]]))
+
+        loop(0, FACE, close_a)
 
     dot_lane = lax.broadcasted_iota(jnp.int32, (8, 128), 1)
 
-    def dot_copies(number, stage):
-        stride, size = GROUPS[stage]
-        return [pltpu.make_async_remote_copy(
-            src_ref=dot_send.at[number, stage], dst_ref=dot_recv.at[number, stage, step - 1],
-            send_sem=dot_ssem.at[number, stage], recv_sem=dot_rsem.at[number, stage],
-            device_id=(partner(stride, size, step),), device_id_type=MESH) for step in range(1, size)]
+    def dot_slots(number, stage):
+        return dot_recv.at[number, pl.ds(FIRST_SLOT[stage], FIRST_SLOT[stage + 1] - FIRST_SLOT[stage])]
 
     def dot_start(number, stage, value):
         dot_send[number, stage] = value
-        for c in dot_copies(number, stage):
-            c.start()
+        for i, device in enumerate(partners(stage)):
+            pltpu.make_async_remote_copy(
+                src_ref=dot_send.at[number, stage], dst_ref=dot_recv.at[number, FIRST_SLOT[stage] + i],
+                send_sem=dot_ssem.at[number, stage], recv_sem=dot_rsem.at[number, stage],
+                device_id=(device,), device_id_type=MESH).start()
 
     def dot_finish(number, stage):
-        slots = dot_recv.at[number, stage]
+        slots = dot_slots(number, stage)
         pltpu.make_async_copy(slots, slots, dot_rsem.at[number, stage]).wait()
-        return dot_send[number, stage] + jnp.sum(dot_recv[number, stage], axis=0)
+        got = dot_recv[number, FIRST_SLOT[stage]:FIRST_SLOT[stage + 1]]
+        return dot_send[number, stage] + jnp.sum(got, axis=0)
 
     def dot_pack(first, second):
         first = jnp.sum(first, axis=1, keepdims=True)
@@ -316,36 +411,53 @@
         split(packed_w, e, v)
 
     loop(0, ROWS, load_rhs, 16)
-    for c in range(ROWS // G_CHUNK):
-        convert_g(c)
     pl.semaphore_wait(barrier, greeted)
+    send_top(0, r0)
 
     def gz_copy():
         return pltpu.make_async_remote_copy(src_ref=gz_send, dst_ref=gz_recv, send_sem=gz_ssem, recv_sem=gz_rsem,
                                             device_id=(below,), device_id_type=MESH)
 
+    def g0_copy():
+        return pltpu.make_async_remote_copy(src_ref=g0_send, dst_ref=g0_recv, send_sem=g0_ssem, recv_sem=g0_rsem,
+                                            device_id=(below,), device_id_type=MESH)
+
     def fill_gz(j):
         gz_send[j] = jnp.concatenate([g_in[place[2 * j], 3], g_in[place[2 * j + 1], 3]], axis=1)
 
+    def fill_g0(j):
+        pair = [g_in[place[(2 * j + s) // 3], (2 * j + s) % 3] for s in range(2)]
+        g0_send[j] = jnp.concatenate(pair, axis=1)
+
+    def split_pairs(received, ref, pairs):
+        def one(j):
+            v = received[j]
+            ref[2 * j] = split_block(v[:, :DOFS])
+            ref[2 * j + 1] = split_block(v[:, DOFS:])
+
+        loop(0, pairs, one)
+
+    chunks = ROWS // G_CHUNK
+    for c in range(chunks):
+        g_copy(c).wait()
+        if c == chunks - 1:
+            loop(0, FACE // 2, fill_gz)
+            gz_copy().start()
+        convert_g(c)
+
     def first_side():
-        loop(0, FACE // 2, fill_gz)
-        gz_copy().start()
+        loop(0, FACE * 3 // 2, fill_g0)
+        g0_copy().start()
         for c in range(ROWS // A_CHUNK - 2):
             convert_a(c)
         gz_copy().wait_recv()
-
-        def one(j):
-            v = gz_recv[j]
-            gz_w[2 * j] = split_block(v[:, :DOFS])
-            gz_w[2 * j + 1] = split_block(v[:, DOFS:])
-
-        loop(0, FACE // 2, one)
+        split_pairs(gz_recv, gz_w, FACE // 2)
 
     def second_side():
         for c in range(ROWS // A_CHUNK - 2, ROWS // A_CHUNK):
             convert_a(c)
 
-    product(0, r0, u0, w0, first_side, second_side)
+    first_product(r0, u0, w0, first_side, second_side)
 
     def dots0(e, carry):
         split(packed_w, e, w0[e])
@@ -354,15 +466,15 @@
     value = dot_pack(*lax.fori_loop(0, ROWS, dots0, (zero, zero), unroll=16))
     dot_start(0, 0, value)
 
-    def middle(number):
-        def run():
-            dot_start(number, 1, dot_finish(number, 0))
-        return run
-
-    def nothing():
-        pass
-
-    product(1, w0, m0, n0, nothing, middle(0))
+    def beside1():
+        dot_start(0, 1, dot_finish(0, 0))
+        g0_copy().wait_recv()
+        split_pairs(g0_recv, g0_w, FACE * 3 // 2)
+
+    def beside2():
+        dot_start(1, 1, dot_finish(1, 0))
+
+    later_product(1, w0, m0, n0, beside1)
     gam0, del0 = dot_unpack(dot_finish(0, 1))
     alpha0 = gam0 / del0
     al0 = jnp.broadcast_to(alpha0, (RHS, 128))
@@ -379,7 +491,7 @@
     value = dot_pack(*lax.fori_loop(0, ROWS, update0, (zero, zero), unroll=16))
     dot_start(1, 0, value)
 
-    product(2, w1, m1, n1, nothing, middle(1))
+    later_product(2, w1, m1, n1, beside2)
     gam1, del1 = dot_unpack(dot_finish(1, 1))
     beta1 = gam1 / gam0
     alpha1 = gam1 / (del1 - beta1 * gam1 / alpha0)
@@ -399,61 +511,54 @@
     value = dot_pack(*lax.fori_loop(0, ROWS, update1, (zero, zero), unroll=16))
     dot_start(2, 0, value)
 
-    def prepare(e):
+    def prepare(i):
+        e = inverse[0, i]
         u, w = u0[e], w0[e]
         v, q = u1[e], w1[e]
-        m0[e] = k0 * u + al1 * v
-        u0[e] = v + be1 * u
-        n0[e] = r0[e] - (k0 * w + al1 * q)
-        w0[e] = q + be1 * w
+        for k, part in enumerate((k0 * u + al1 * v, m1[e], v + be1 * u, r0[e] - (k0 * w + al1 * q), n1[e], q + be1 * w)):
+            parts[k, i] = part[:, :DOFS]
 
     loop(0, ROWS, prepare, 16)
+    parts_copy = pltpu.make_async_copy(parts, parts_hbm, out_sem.at[0])
+    parts_copy.start()
     dot_start(2, 1, dot_finish(2, 0))
     gam2, del2 = dot_unpack(dot_finish(2, 1))
     beta2 = gam2 / gam1
     alpha2 = gam2 / (del2 - beta2 * gam2 / alpha1)
-    al2 = jnp.broadcast_to(alpha2, (RHS, 128))
-    ab2 = jnp.broadcast_to(alpha2 * beta2, (RHS, 128))
-
-    def finish_x(i):
-        e = inverse[0, i]
-        x_out[i] = (m0[e] + (al2 * m1[e] + ab2 * u0[e]))[:, :DOFS]
-
-    def finish_r(i):
-        e = inverse[0, i]
-        r_out[i] = (n0[e] - (al2 * n1[e] + ab2 * w0[e]))[:, :DOFS]
-
-    loop(0, ROWS, finish_x, 16)
-    x_copy = pltpu.make_async_copy(x_out, x_hbm, out_sem.at[0])
-    x_copy.start()
-    loop(0, ROWS, finish_r, 16)
-    r_copy = pltpu.make_async_copy(r_out, r_hbm, out_sem.at[1])
-    r_copy.start()
-    x_copy.wait()
-    r_copy.wait()
+    coef[0] = jnp.broadcast_to(alpha2, (RHS, DOFS))
+    coef[1] = jnp.broadcast_to(alpha2 * beta2, (RHS, DOFS))
+    ends = [parts_copy]
+    for k, ref in enumerate((alpha_hbm, alpha_beta_hbm)):
+        ends.append(pltpu.make_async_copy(coef.at[k], ref, out_sem.at[1 + k]))
+        ends[-1].start()
+    for c in ends:
+        c.wait()
 
     gz_copy().wait_send()
+    g0_copy().wait_send()
     for slot in range(12):
         halo_copy(slot).wait_send()
     for number in range(3):
         for stage in range(2):
-            slots = dot_recv.at[number, stage]
+            slots = dot_slots(number, stage)
             pltpu.make_async_copy(slots, slots, dot_ssem.at[number, stage]).wait()
 
 
 def body(right_side, a_blocks, a_cols, g_blocks, g_cols, send_up, send_down):
     field = pltpu.VMEM((ROWS, RHS, 128), F32)
     packed = pltpu.VMEM((ROWS, 2 * RHS, 128), BF16)
+    edge = pltpu.VMEM((FACE, RHS, 128), F32)
     face = pltpu.VMEM((FACE, 2 * RHS, 128), BF16)
     hbm = pl.BlockSpec(memory_space=pl.ANY)
     smem = pl.BlockSpec(memory_space=pltpu.SMEM)
     dma = pltpu.SemaphoreType.DMA
-    out = jax.ShapeDtypeStruct((ROWS, RHS, DOFS), F32)
-    return pl.pallas_call(
+    pairs = FACE // 2
+    small = jax.ShapeDtypeStruct((RHS, DOFS), F32)
+    parts, alpha, alpha_beta = pl.pallas_call(
         kernel,
-        out_shape=(out, out),
+        out_shape=(jax.ShapeDtypeStruct((6, ROWS, RHS, DOFS), F32), small, small),
         in_specs=[hbm, hbm, hbm, smem, smem, smem],
-        out_specs=(hbm, hbm),
+        out_specs=(hbm, hbm, hbm),
         scratch_shapes=[
             pltpu.VMEM((ROWS, RHS, DOFS), F32),
             pltpu.VMEM((A_SLOTS, A_CHUNK, 7, DOFS, DOFS), F32),
@@ -461,31 +566,37 @@
             pltpu.VMEM((ROWS * 7, DOFS, 128), BF16),
             pltpu.VMEM((ROWS * 4, DOFS, 128), BF16),
             pltpu.VMEM((FACE, DOFS, 128), BF16),
+            pltpu.VMEM((FACE * 3, DOFS, 128), BF16),
             packed, packed, packed,
-            face, face, face, face,
-            pltpu.VMEM((FACE, RHS, 128), F32),
-            pltpu.VMEM((FACE, RHS, 128), F32),
+            face, face, face, face, face, face,
+            edge, edge, edge, edge,
             field, field, field, field, field, field, field, field, field,
-            pltpu.VMEM((ROWS, RHS, DOFS), F32),
-            pltpu.VMEM((ROWS, RHS, DOFS), F32),
-            pltpu.VMEM((FACE // 2, DOFS, 128), F32),
-            pltpu.VMEM((FACE // 2, DOFS, 128), F32),
+            pltpu.VMEM((6, ROWS, RHS, DOFS), F32),
+            pltpu.VMEM((2, RHS, DOFS), F32),
+            pltpu.VMEM((pairs, DOFS, 128), F32),
+            pltpu.VMEM((pairs, DOFS, 128), F32),
+            pltpu.VMEM((pairs * 3, DOFS, 128), F32),
+            pltpu.VMEM((pairs * 3, DOFS, 128), F32),
             pltpu.VMEM((12, FACE // 2, RHS, 128), F32),
             pltpu.VMEM((12, FACE // 2, RHS, 128), F32),
             pltpu.VMEM((3, 2, 8, 128), F32),
-            pltpu.VMEM((3, 2, 15, 8, 128), F32),
+            pltpu.VMEM((3, FIRST_SLOT[2], 8, 128), F32),
             pltpu.SMEM((ROWS,), jnp.int32),
             pltpu.SMEM((8, 128), jnp.int32),
             pltpu.SMEM((ROWS * 4,), jnp.int32),
             pltpu.SMEM((FACE,), jnp.int32),
             pltpu.SMEM((FACE,), jnp.int32),
+            pltpu.SMEM((2 * FACE,), jnp.int32),
+            pltpu.SMEM((2 * FACE,), jnp.int32),
             pltpu.VMEM((8, 128), jnp.int32),
-            dma((5,)), dma((A_SLOTS,)), dma((2,)), dma, dma, dma,
+            dma((5,)), dma((A_SLOTS,)), dma((3,)), dma, dma, dma, dma, dma,
             dma((12,)), dma((12,)), dma((3, 2)), dma((3, 2)),
         ],
         compiler_params=pltpu.CompilerParams(
             collective_id=0, has_side_effects=True, vmem_limit_bytes=60 * 2 ** 20),
     )(right_side, a_blocks, g_blocks, a_cols.T, send_up, send_down)
+    return (parts[0] + (alpha * parts[1] + alpha_beta * parts[2]),
+            parts[3] - (alpha * parts[4] + alpha_beta * parts[5]))
 
 
 def solution(mesh):

time: 78.5 us -> 74.8 us (0.953)
  other arithmetic: 0 us -> 4.9 us
  local copies, waits for them, and re-layouts: 4.52 us -> 0 us
  Pallas kernels: 73.1 us -> 69.2 us
    sub x0 -> x1, other arithmetic: none -> 4.9 us  [body(): parts[3] - (alpha * parts[4] + alpha_beta * parts[5])]
    unnamed x2 -> x0, local copies, waits for them, and re-layouts: 4.52 us -> none
    pallas_call x1, Pallas kernels: 73.1 us -> 69.2 us  [body(): pl.pallas_call(kernel, out_shape=(jax.ShapeDtypeStruct((6, ROWS, RHS, DOF...]
where the time goes in v2:
time: 74.8 us; the launch traced here: 74.7 us
  Pallas kernels  69.2 us (93%)
  other arithmetic  4.9 us (7%)
    pallas_call x1, Pallas kernels, body(): pl.pallas_call(kernel, out_shape=(jax.ShapeDtypeStruct((6, ROWS, RHS, DOF...  69.2 us
    sub x1, other arithmetic, body(): parts[3] - (alpha * parts[4] + alpha_beta * parts[5])  4.9 us

profile of v2, /device:TPU:1, one launch (start us, length us, event | category | flops | bytes accessed | tf_op | source)
XLA Modules:
  0.0 74.7 jit_solution(15043855192992162413)
XLA Ops:
  0.6 69.2 %shard_map.77 = (f32[6,64,32,64]{3,2,1,0:T(8,128)}, f32[32,64]{1,0:T(8,128)}, f32[32,64]{1,0:T(8,128)}) custom-call(f32[64,32,64]{2,1,0:T(8,128)} %rhs_hbm.1, f32[64,7,64,64]{3,2,1,0:T(8,128)} %a_hbm.1, f32[64,4,64,64]{3,2,1,0:T(8,128)} %g_hbm.1, s32[6,64]{1,0:T(8,128)} %bitcast.25, s32[1,16]{1,0:T(1,128)} %send_up.1, s32[1,16]{1,0:T(1,128)} %send_down.1), custom_call_target="tpu_custom_call" | custom-call | tf_op jit(solution)/shard_map/pallas_call | solution.py:557
  69.8 4.9 %fusion.1 = (f32[64,32,64]{2,1,0:T(8,128)}, f32[64,32,64]{2,1,0:T(8,128)}) fusion(f32[6,64,32,64]{3,2,1,0:T(8,128)} %get-tuple-element.5, f32[32,64]{1,0:T(8,128)} %get-tuple-element.7, f32[32,64]{1,0:T(8,128)} %get-tuple-element.6), kind=kLoop, calls=%fused_computation.2 | loop fusion | flops 1048576 | bytes 4210688 | tf_op jit(solution)/shard_map/sub | solution.py:599

commit v3 on v2

--- a/solution.py
+++ b/solution.py
@@ -21,6 +21,7 @@
 A_SLOTS = 4
 GROUPS = (((1, 2), (2, 4), (64, 4)), ((8, 8),))
 FIRST_SLOT = (0, 31, 38)
+LAST_CHUNKS = 4
 
 
 def loop(lo, hi, fn, unroll=None):
@@ -31,12 +32,12 @@
     lax.fori_loop(lo, hi, step, 0, unroll=(hi - lo) if unroll is None else unroll)
 
 
-def kernel(rhs_hbm, a_hbm, g_hbm, cols, send_up, send_down, parts_hbm, alpha_hbm, alpha_beta_hbm,
+def kernel(rhs_hbm, a_hbm, g_hbm, cols, send_up, send_down, parts_hbm, coef_hbm,
            rhs_in, a_in, g_in, a_w, g_w, gz_w, g0_w, packed_w, packed_y, packed_m,
-           low_w, high_y, low_m, high_m, low_t, high_t, y_loc, y_far, u_low, u_high,
+           low_w, high_y, low_m, high_m, y_loc, y_far, u_low, u_high,
            r0, u0, w0, m0, n0, u1, w1, m1, n1, parts, coef,
            gz_send, gz_recv, g0_send, g0_recv, halo_send, halo_recv, dot_send, dot_recv,
-           place, inverse, near, low_at, high_at, low_side, high_side, inverse_vec,
+           place, inverse, near, low_at, high_at, high_side, inverse_vec,
            in_sem, a_sem, out_sem, tab_sem, gz_ssem, gz_rsem, g0_ssem, g0_rsem, halo_ssem, halo_rsem, dot_ssem, dot_rsem):
     count = lax.axis_size("dom")
     me = lax.axis_index("dom")
@@ -109,7 +110,6 @@
         high_at[h] = jnp.clip(cols[5, place[3 * FACE + h]] - (ROWS + FACE), 0, FACE - 1)
 
         for s in range(2):
-            low_side[h * 2 + s] = jnp.clip(near[h * 4 + 1 + 2 * s], 0, FACE - 1)
             high_side[h * 2 + s] = jnp.clip(near[(3 * FACE + h) * 4 + 1 + 2 * s] - 3 * FACE, 0, FACE - 1)
 
     loop(0, FACE, crossings, 4)
@@ -221,15 +221,13 @@
 
     def bottom(h):
         row = place[h] * 4
-        v = twice(times([packed_w[h], packed_w[near[h * 4]], packed_w[near[h * 4 + 2]]],
-                        [g_w[row], g_w[row + 1], g_w[row + 2]]))
-        y_loc[h] = v
-        split(packed_y, h, v)
+        y_loc[h] = twice(times([packed_w[h], packed_w[near[h * 4]], packed_w[near[h * 4 + 2]]],
+                               [g_w[row], g_w[row + 1], g_w[row + 2]]))
 
     def inner_y(e):
         split(packed_y, e, twice(row_y(e, packed_w[e - FACE])))
 
-    def first_product(field, out_m, out_n, beside_first, beside_second):
+    def first_product(out_m, out_n, beside_first, beside_inner, beside_second):
         loop(0, FACE, bottom)
         send_bottom(1, y_loc)
         beside_first()
@@ -243,6 +241,7 @@
             put_u(e, row_u(e, packed_y[e + FACE], g_w[place[e + FACE] * 4 + 3]))
 
         loop(FACE, 3 * FACE, inner_u)
+        beside_inner()
         halo_copy(0).wait_recv()
         halo_copy(1).wait_recv()
         unpack_split(0, low_w)
@@ -283,25 +282,27 @@
 
         loop(0, FACE, outer_a)
 
-    def later_product(number, field, out_m, out_n, beside):
+    def later_product(number, out_m, out_n, beside):
         base = number * 4
-        send_top(base, field)
-        loop(0, FACE, bottom)
-        send_bottom(base + 1, y_loc)
-        loop(FACE, 2 * FACE, inner_y)
-        loop(3 * FACE, ROWS, inner_y)
-
-        def part_u(h):
-            out_m[h] = row_u(h, packed_y[h + FACE], g_w[place[h + FACE] * 4 + 3])
+
+        def part_high(h):
             e = 3 * FACE + h
             ex = near[e * 4 + 1]
             ey = near[e * 4 + 3]
             out_m[e] = times_transposed([packed_y[e], packed_y[ex], packed_y[ey]],
                                         [g_w[place[e] * 4], g_w[place[ex] * 4 + 1], g_w[place[ey] * 4 + 2]])
 
-        loop(0, FACE, part_u)
+        def part_low(h):
+            out_m[h] = times_transposed([packed_y[h + FACE]], [g_w[place[h + FACE] * 4 + 3]])
+
+        loop(3 * FACE, ROWS, inner_y)
+        loop(0, FACE, part_high)
+        send_top(base + 2, out_m)
+        loop(0, FACE, bottom)
+        send_bottom(base + 1, y_loc)
+        loop(FACE, 2 * FACE, inner_y)
+        loop(0, FACE, part_low)
         send_bottom(base + 3, out_m)
-        send_top(base + 2, out_m)
         loop(2 * FACE, 3 * FACE, inner_y)
 
         def put_u(e, v):
@@ -323,52 +324,61 @@
 
         loop(0, FACE, part_a)
         beside()
+
         halo_copy(base).wait_recv()
+        unpack_split(base, low_w)
+        halo_copy(base + 2).wait_recv()
+        unpack(base + 2, u_low)
+
+        def close_y_low(h):
+            extra = twice(times([low_w[low_at[h]]], [g_w[place[h] * 4 + 3]]))
+            split(packed_y, h, y_loc[h] + extra)
+
+        def close_u_low(h):
+            ex, ey = near[h * 4 + 1], near[h * 4 + 3]
+            put_u(h, out_m[h] + times_transposed(
+                [packed_y[h], packed_y[ex], packed_y[ey]],
+                [g_w[place[h] * 4], g_w[place[ex] * 4 + 1], g_w[place[ey] * 4 + 2]]))
+            split(low_m, h, u_low[low_at[h]] + times_transposed([packed_y[h]], [g_w[place[h] * 4 + 3]]))
+
+        def close_a_low(h):
+            out_n[h] = row_a(h, low_m[h], packed_m[h + FACE])
+            e = FACE + h
+            out_n[e] = out_n[e] + twice(times([packed_m[h]], [a_w[place[e] * 7 + 5]]))
+
+        loop(0, FACE, close_y_low)
+        loop(0, FACE, close_u_low)
+        loop(0, FACE, close_a_low)
+
         halo_copy(base + 1).wait_recv()
-        unpack_split(base, low_w)
+        halo_copy(base + 3).wait_recv()
         unpack(base + 1, y_far)
-
-        def close_y(h):
-            extra = twice(times([low_w[low_at[h]]], [g_w[place[h] * 4 + 3]]))
-            split(low_t, h, extra)
-            split(packed_y, h, y_loc[h] + extra)
-            t = high_at[h]
-            more = twice(times([packed_w[3 * FACE + h]], [gz_w[t]]))
-            split(high_t, h, more)
-            split(high_y, h, y_far[t] + more)
-
-        loop(0, FACE, close_y)
-        halo_copy(base + 2).wait_recv()
-        halo_copy(base + 3).wait_recv()
-        unpack(base + 2, u_low)
         unpack(base + 3, u_high)
 
-        def close_u(h):
-            ex, ey = low_side[2 * h], low_side[2 * h + 1]
-            put_u(h, out_m[h] + times_transposed(
-                [low_t[h], low_t[ex], low_t[ey]],
-                [g_w[place[h] * 4], g_w[place[ex] * 4 + 1], g_w[place[ey] * 4 + 2]]))
+        def close_y_high(h):
+            more = twice(times([packed_w[3 * FACE + h]], [gz_w[high_at[h]]]))
+            split(high_y, h, y_far[high_at[h]] + more)
+
+        def close_u_high(h):
             e = 3 * FACE + h
             put_u(e, out_m[e] + times_transposed([high_y[h]], [gz_w[high_at[h]]]))
-            split(low_m, h, u_low[low_at[h]] + times_transposed([packed_y[h]], [g_w[place[h] * 4 + 3]]))
             hx, hy = high_side[2 * h], high_side[2 * h + 1]
             split(high_m, h, u_high[high_at[h]] + times_transposed(
-                [high_t[h], high_t[hx], high_t[hy]],
+                [high_y[h], high_y[hx], high_y[hy]],
                 [g0_w[high_at[h] * 3], g0_w[high_at[hx] * 3 + 1], g0_w[high_at[hy] * 3 + 2]]))
 
-        loop(0, FACE, close_u)
-
-        def close_a(h):
-            out_n[h] = row_a(h, low_m[h], packed_m[h + FACE])
+        def close_a_high(h):
             e = 3 * FACE + h
             out_n[e] = row_a(e, packed_m[e - FACE], high_m[h])
-            for layer, k, other in ((1, 5, 0), (2, 6, 3)):
-                e = layer * FACE + h
-                out_n[e] = out_n[e] + twice(times([packed_m[other * FACE + h]], [a_w[place[e] * 7 + k]]))
-
-        loop(0, FACE, close_a)
-
-    dot_lane = lax.broadcasted_iota(jnp.int32, (8, 128), 1)
+            e = 2 * FACE + h
+            out_n[e] = out_n[e] + twice(times([packed_m[e + FACE]], [a_w[place[e] * 7 + 6]]))
+
+        loop(0, FACE, close_y_high)
+        loop(0, FACE, close_u_high)
+        loop(0, FACE, close_a_high)
+
+    dot_lane = lax.broadcasted_iota(jnp.int32, (RHS, 128), 1)
+    dot_row = lax.broadcasted_iota(jnp.int32, (RHS, 128), 0)
 
     def dot_slots(number, stage):
         return dot_recv.at[number, pl.ds(FIRST_SLOT[stage], FIRST_SLOT[stage + 1] - FIRST_SLOT[stage])]
@@ -390,15 +400,12 @@
     def dot_pack(first, second):
         first = jnp.sum(first, axis=1, keepdims=True)
         second = jnp.sum(second, axis=1, keepdims=True)
-        out = jnp.zeros((8, 128), F32)
-        for g in range(4):
-            out = jnp.where(dot_lane == 2 * g, first[8 * g:8 * g + 8], out)
-            out = jnp.where(dot_lane == 2 * g + 1, second[8 * g:8 * g + 8], out)
-        return out
+        spread = jnp.where(dot_lane == dot_row, first, jnp.where(dot_lane == dot_row + RHS, second, 0.0))
+        return jnp.sum(spread, axis=0, keepdims=True)
 
     def dot_unpack(v):
-        first = jnp.concatenate([v[:, 2 * g:2 * g + 1] for g in range(4)], axis=0)
-        second = jnp.concatenate([v[:, 2 * g + 1:2 * g + 2] for g in range(4)], axis=0)
+        first = jnp.sum(jnp.where(dot_lane == dot_row, v, 0.0), axis=1, keepdims=True)
+        second = jnp.sum(jnp.where(dot_lane == dot_row + RHS, v, 0.0), axis=1, keepdims=True)
         return first, second
 
     zero = jnp.zeros((RHS, 128), F32)
@@ -447,9 +454,13 @@
 
     def first_side():
         loop(0, FACE * 3 // 2, fill_g0)
-        g0_copy().start()
         for c in range(ROWS // A_CHUNK - 2):
             convert_a(c)
+
+    def inner_side():
+        halo_copy(1).wait_send()
+        gz_copy().wait_send()
+        g0_copy().start()
         gz_copy().wait_recv()
         split_pairs(gz_recv, gz_w, FACE // 2)
 
@@ -457,7 +468,8 @@
         for c in range(ROWS // A_CHUNK - 2, ROWS // A_CHUNK):
             convert_a(c)
 
-    first_product(r0, u0, w0, first_side, second_side)
+    first_product(u0, w0, first_side, inner_side, second_side)
+    send_top(4, w0)
 
     def dots0(e, carry):
         split(packed_w, e, w0[e])
@@ -474,7 +486,7 @@
     def beside2():
         dot_start(1, 1, dot_finish(1, 0))
 
-    later_product(1, w0, m0, n0, beside1)
+    later_product(1, m0, n0, beside1)
     gam0, del0 = dot_unpack(dot_finish(0, 1))
     alpha0 = gam0 / del0
     al0 = jnp.broadcast_to(alpha0, (RHS, 128))
@@ -488,10 +500,11 @@
         split(packed_w, e, w)
         return carry[0] + r * u, carry[1] + w * u
 
-    value = dot_pack(*lax.fori_loop(0, ROWS, update0, (zero, zero), unroll=16))
-    dot_start(1, 0, value)
-
-    later_product(2, w1, m1, n1, beside2)
+    sums = lax.fori_loop(3 * FACE, ROWS, update0, (zero, zero), unroll=16)
+    send_top(8, w1)
+    dot_start(1, 0, dot_pack(*lax.fori_loop(0, 3 * FACE, update0, sums, unroll=16)))
+
+    later_product(2, m1, n1, beside2)
     gam1, del1 = dot_unpack(dot_finish(1, 1))
     beta1 = gam1 / gam0
     alpha1 = gam1 / (del1 - beta1 * gam1 / alpha0)
@@ -511,37 +524,68 @@
     value = dot_pack(*lax.fori_loop(0, ROWS, update1, (zero, zero), unroll=16))
     dot_start(2, 0, value)
 
-    def prepare(i):
-        e = inverse[0, i]
+    def prepare(e):
         u, w = u0[e], w0[e]
         v, q = u1[e], w1[e]
-        for k, part in enumerate((k0 * u + al1 * v, m1[e], v + be1 * u, r0[e] - (k0 * w + al1 * q), n1[e], q + be1 * w)):
-            parts[k, i] = part[:, :DOFS]
-
-    loop(0, ROWS, prepare, 16)
+        return k0 * u + al1 * v, m1[e], v + be1 * u, r0[e] - (k0 * w + al1 * q), n1[e], q + be1 * w
+
+    def prepare_pair(j):
+        for k, (a, b) in enumerate(zip(prepare(inverse[0, 2 * j]), prepare(inverse[0, 2 * j + 1]))):
+            parts[k, j] = jnp.where(left, a, b)
+
+    loop(0, ROWS // 2, prepare_pair, 8)
     parts_copy = pltpu.make_async_copy(parts, parts_hbm, out_sem.at[0])
     parts_copy.start()
     dot_start(2, 1, dot_finish(2, 0))
     gam2, del2 = dot_unpack(dot_finish(2, 1))
     beta2 = gam2 / gam1
     alpha2 = gam2 / (del2 - beta2 * gam2 / alpha1)
-    coef[0] = jnp.broadcast_to(alpha2, (RHS, DOFS))
-    coef[1] = jnp.broadcast_to(alpha2 * beta2, (RHS, DOFS))
-    ends = [parts_copy]
-    for k, ref in enumerate((alpha_hbm, alpha_beta_hbm)):
-        ends.append(pltpu.make_async_copy(coef.at[k], ref, out_sem.at[1 + k]))
-        ends[-1].start()
-    for c in ends:
-        c.wait()
-
-    gz_copy().wait_send()
+    coef[0] = jnp.broadcast_to(alpha2, (RHS, 128))
+    coef[1] = jnp.broadcast_to(alpha2 * beta2, (RHS, 128))
+    coef_copy = pltpu.make_async_copy(coef, coef_hbm, out_sem.at[1])
+    coef_copy.start()
+    parts_copy.wait()
+    coef_copy.wait()
+
     g0_copy().wait_send()
     for slot in range(12):
-        halo_copy(slot).wait_send()
+        if slot != 1:
+            halo_copy(slot).wait_send()
     for number in range(3):
         for stage in range(2):
             slots = dot_slots(number, stage)
             pltpu.make_async_copy(slots, slots, dot_ssem.at[number, stage]).wait()
+
+
+def finish(parts_hbm, coef_hbm, x_hbm, r_hbm, parts, coef, x_out, r_out, in_sem, coef_sem, out_sem):
+    size = ROWS // 2 // LAST_CHUNKS
+    coef_copy = pltpu.make_async_copy(coef_hbm, coef, coef_sem)
+    coef_copy.start()
+    copies = []
+    for c in range(LAST_CHUNKS):
+        part = pl.ds(c * size, size)
+        copies.append(pltpu.make_async_copy(parts_hbm.at[:, part], parts.at[:, part], in_sem.at[c]))
+        copies[-1].start()
+    coef_copy.wait()
+    alpha, alpha_beta = coef[0], coef[1]
+    ends = []
+    for c in range(LAST_CHUNKS):
+        copies[c].wait()
+
+        def one(j):
+            x = parts[0, j] + (alpha * parts[1, j] + alpha_beta * parts[2, j])
+            r = parts[3, j] - (alpha * parts[4, j] + alpha_beta * parts[5, j])
+            for ref, v in ((x_out, x), (r_out, r)):
+                ref[2 * j] = v[:, :DOFS]
+                ref[2 * j + 1] = v[:, DOFS:]
+
+        loop(c * size, (c + 1) * size, one)
+        rows = pl.ds(2 * c * size, 2 * size)
+        for k, (ref, hbm) in enumerate(((x_out, x_hbm), (r_out, r_hbm))):
+            ends.append(pltpu.make_async_copy(ref.at[rows], hbm.at[rows], out_sem.at[k, c]))
+            ends[-1].start()
+    for c in ends:
+        c.wait()
 
 
 def body(right_side, a_blocks, a_cols, g_blocks, g_cols, send_up, send_down):
@@ -553,12 +597,11 @@
     smem = pl.BlockSpec(memory_space=pltpu.SMEM)
     dma = pltpu.SemaphoreType.DMA
     pairs = FACE // 2
-    small = jax.ShapeDtypeStruct((RHS, DOFS), F32)
-    parts, alpha, alpha_beta = pl.pallas_call(
+    parts, coef = pl.pallas_call(
         kernel,
-        out_shape=(jax.ShapeDtypeStruct((6, ROWS, RHS, DOFS), F32), small, small),
+        out_shape=(jax.ShapeDtypeStruct((6, ROWS // 2, RHS, 128), F32), jax.ShapeDtypeStruct((2, RHS, 128), F32)),
         in_specs=[hbm, hbm, hbm, smem, smem, smem],
-        out_specs=(hbm, hbm, hbm),
+        out_specs=(hbm, hbm),
         scratch_shapes=[
             pltpu.VMEM((ROWS, RHS, DOFS), F32),
             pltpu.VMEM((A_SLOTS, A_CHUNK, 7, DOFS, DOFS), F32),
@@ -568,35 +611,47 @@
             pltpu.VMEM((FACE, DOFS, 128), BF16),
             pltpu.VMEM((FACE * 3, DOFS, 128), BF16),
             packed, packed, packed,
-            face, face, face, face, face, face,
+            face, face, face, face,
             edge, edge, edge, edge,
             field, field, field, field, field, field, field, field, field,
-            pltpu.VMEM((6, ROWS, RHS, DOFS), F32),
-            pltpu.VMEM((2, RHS, DOFS), F32),
+            pltpu.VMEM((6, ROWS // 2, RHS, 128), F32),
+            pltpu.VMEM((2, RHS, 128), F32),
             pltpu.VMEM((pairs, DOFS, 128), F32),
             pltpu.VMEM((pairs, DOFS, 128), F32),
             pltpu.VMEM((pairs * 3, DOFS, 128), F32),
             pltpu.VMEM((pairs * 3, DOFS, 128), F32),
             pltpu.VMEM((12, FACE // 2, RHS, 128), F32),
             pltpu.VMEM((12, FACE // 2, RHS, 128), F32),
-            pltpu.VMEM((3, 2, 8, 128), F32),
-            pltpu.VMEM((3, FIRST_SLOT[2], 8, 128), F32),
+            pltpu.VMEM((3, 2, 1, 128), F32),
+            pltpu.VMEM((3, FIRST_SLOT[2], 1, 128), F32),
             pltpu.SMEM((ROWS,), jnp.int32),
             pltpu.SMEM((8, 128), jnp.int32),
             pltpu.SMEM((ROWS * 4,), jnp.int32),
             pltpu.SMEM((FACE,), jnp.int32),
             pltpu.SMEM((FACE,), jnp.int32),
             pltpu.SMEM((2 * FACE,), jnp.int32),
-            pltpu.SMEM((2 * FACE,), jnp.int32),
             pltpu.VMEM((8, 128), jnp.int32),
-            dma((5,)), dma((A_SLOTS,)), dma((3,)), dma, dma, dma, dma, dma,
+            dma((5,)), dma((A_SLOTS,)), dma((2,)), dma, dma, dma, dma, dma,
             dma((12,)), dma((12,)), dma((3, 2)), dma((3, 2)),
         ],
         compiler_params=pltpu.CompilerParams(
             collective_id=0, has_side_effects=True, vmem_limit_bytes=60 * 2 ** 20),
     )(right_side, a_blocks, g_blocks, a_cols.T, send_up, send_down)
-    return (parts[0] + (alpha * parts[1] + alpha_beta * parts[2]),
-            parts[3] - (alpha * parts[4] + alpha_beta * parts[5]))
+    out = jax.ShapeDtypeStruct((ROWS, RHS, DOFS), F32)
+    return pl.pallas_call(
+        finish,
+        out_shape=(out, out),
+        in_specs=[hbm, hbm],
+        out_specs=(hbm, hbm),
+        scratch_shapes=[
+            pltpu.VMEM((6, ROWS // 2, RHS, 128), F32),
+            pltpu.VMEM((2, RHS, 128), F32),
+            pltpu.VMEM((ROWS, RHS, DOFS), F32),
+            pltpu.VMEM((ROWS, RHS, DOFS), F32),
+            dma((LAST_CHUNKS,)), dma, dma((2, LAST_CHUNKS)),
+        ],
+        compiler_params=pltpu.CompilerParams(vmem_limit_bytes=60 * 2 ** 20),
+    )(parts, coef)
 
 
 def solution(mesh):

time: 74.8 us -> 70.3 us (0.940)
  other arithmetic: 4.9 us -> 0 us
    sub x1 -> x0, other arithmetic: 4.9 us -> none  [body(): parts[3] - (alpha * parts[4] + alpha_beta * parts[5])]
    pallas_call x1 -> x2, Pallas kernels: 69.2 us -> 69.3 us  [the longest x1 66.3 us: body(): pl.pallas_call(kernel, out_shape=(jax.ShapeDtypeStruct((6, ROWS // 2, RHS...]
where the time goes in v3:
time: 70.3 us; the launch traced here: 70.1 us
  Pallas kernels  69.3 us (99%)
  between operations  0.82 us (1%)
    pallas_call x1, Pallas kernels, body(): pl.pallas_call(kernel, out_shape=(jax.ShapeDtypeStruct((6, ROWS // 2, RHS...  66.3 us
    pallas_call x1, Pallas kernels, body(): pl.pallas_call(finish, out_shape=(out, out), in_specs=[hbm, hbm], out_spe...  3.01 us

profile of v3, /device:TPU:1, one launch (start us, length us, event | category | flops | bytes accessed | tf_op | source)
XLA Modules:
  0.0 70.1 jit_solution(11949519405074066647)
XLA Ops:
  0.6 66.3 %shard_map.77 = (f32[6,32,32,128]{3,2,1,0:T(8,128)}, f32[2,32,128]{2,1,0:T(8,128)}) custom-call(f32[64,32,64]{2,1,0:T(8,128)} %rhs_hbm.1, f32[64,7,64,64]{3,2,1,0:T(8,128)} %a_hbm.1, f32[64,4,64,64]{3,2,1,0:T(8,128)} %g_hbm.1, s32[6,64]{1,0:T(8,128)} %bitcast.1, s32[1,16]{1,0:T(1,128)} %send_up.1, s32[1,16]{1,0:T(1,128)} %send_down.1), custom_call_target="tpu_custom_call" | custom-call | tf_op jit(solution)/shard_map/pallas_call | solution.py:600
  66.9 3.0 %shard_map.78 = (f32[64,32,64]{2,1,0:T(8,128)}, f32[64,32,64]{2,1,0:T(8,128)}) custom-call(f32[6,32,32,128]{3,2,1,0:T(8,128)} %get-tuple-element.4.parts_hbm, f32[2,32,128]{2,1,0:T(8,128)} %get-tuple-element.5.coef_hbm), custom_call_target="tpu_custom_call" | custom-call | tf_op jit(solution)/shard_map/pallas_call | solution.py:641

commit v4 on v3

--- a/solution.py
+++ b/solution.py
@@ -241,48 +241,58 @@
             put_u(e, row_u(e, packed_y[e + FACE], g_w[place[e + FACE] * 4 + 3]))
 
         loop(FACE, 3 * FACE, inner_u)
-        beside_inner()
+
         halo_copy(0).wait_recv()
-        halo_copy(1).wait_recv()
         unpack_split(0, low_w)
-        unpack(1, y_far)
-
-        def close_y(h):
+
+        def close_y_low(h):
             extra = times([low_w[low_at[h]]], [g_w[place[h] * 4 + 3]])
             split(packed_y, h, y_loc[h] + twice(extra))
+
+        def outer_u_low(h):
+            put_u(h, row_u(h, packed_y[h + FACE], g_w[place[h + FACE] * 4 + 3]))
+
+        loop(0, FACE, close_y_low)
+        loop(0, FACE, outer_u_low)
+        send_bottom(3, out_m)
+        beside_inner()
+        halo_copy(1).wait_recv()
+        unpack(1, y_far)
+
+        def close_y_high(h):
             t = high_at[h]
             more = times([packed_w[3 * FACE + h]], [gz_w[t]])
             split(high_y, h, y_far[t] + twice(more))
 
-        loop(0, FACE, close_y)
-
-        def outer_u(h):
-            put_u(h, row_u(h, packed_y[h + FACE], g_w[place[h + FACE] * 4 + 3]))
+        def outer_u_high(h):
             e = 3 * FACE + h
             put_u(e, row_u(e, high_y[h], gz_w[high_at[h]]))
 
-        loop(0, FACE, outer_u)
-        send_bottom(3, out_m)
+        loop(0, FACE, close_y_high)
+        loop(0, FACE, outer_u_high)
         send_top(2, out_m)
         beside_second()
 
         def inner_a(e):
             out_n[e] = row_a(e, packed_m[e - FACE], packed_m[e + FACE])
 
-        loop(FACE, 3 * FACE, inner_a)
-        halo_copy(2).wait_recv()
-        halo_copy(3).wait_recv()
-        unpack_split(2, low_m)
-        unpack_split(3, high_m)
-
-        def outer_a(h):
-            out_n[h] = row_a(h, low_m[low_at[h]], packed_m[h + FACE])
+        def outer_a_high(h):
             e = 3 * FACE + h
             out_n[e] = row_a(e, packed_m[e - FACE], high_m[high_at[h]])
 
-        loop(0, FACE, outer_a)
-
-    def later_product(number, out_m, out_n, beside):
+        def outer_a_low(h):
+            out_n[h] = row_a(h, low_m[low_at[h]], packed_m[h + FACE])
+
+        loop(FACE, 3 * FACE, inner_a)
+        halo_copy(3).wait_recv()
+        unpack_split(3, high_m)
+        loop(0, FACE, outer_a_high)
+        send_top(4, out_n)
+        halo_copy(2).wait_recv()
+        unpack_split(2, low_m)
+        loop(0, FACE, outer_a_low)
+
+    def later_product(number, out_m, out_n, start_sum, beside, before_high):
         base = number * 4
 
         def part_high(h):
@@ -298,6 +308,7 @@
         loop(3 * FACE, ROWS, inner_y)
         loop(0, FACE, part_high)
         send_top(base + 2, out_m)
+        start_sum()
         loop(0, FACE, bottom)
         send_bottom(base + 1, y_loc)
         loop(FACE, 2 * FACE, inner_y)
@@ -350,6 +361,8 @@
         loop(0, FACE, close_u_low)
         loop(0, FACE, close_a_low)
 
+        before_high()
+
         halo_copy(base + 1).wait_recv()
         halo_copy(base + 3).wait_recv()
         unpack(base + 1, y_far)
@@ -454,39 +467,44 @@
 
     def first_side():
         loop(0, FACE * 3 // 2, fill_g0)
-        for c in range(ROWS // A_CHUNK - 2):
+        for c in range(4):
             convert_a(c)
 
     def inner_side():
         halo_copy(1).wait_send()
         gz_copy().wait_send()
         g0_copy().start()
+        for c in range(4, 6):
+            convert_a(c)
         gz_copy().wait_recv()
         split_pairs(gz_recv, gz_w, FACE // 2)
 
     def second_side():
-        for c in range(ROWS // A_CHUNK - 2, ROWS // A_CHUNK):
+        for c in range(6, ROWS // A_CHUNK):
             convert_a(c)
 
     first_product(u0, w0, first_side, inner_side, second_side)
-    send_top(4, w0)
 
     def dots0(e, carry):
         split(packed_w, e, w0[e])
         return carry[0] + r0[e] * u0[e], carry[1] + w0[e] * u0[e]
 
-    value = dot_pack(*lax.fori_loop(0, ROWS, dots0, (zero, zero), unroll=16))
-    dot_start(0, 0, value)
+    sums0 = lax.fori_loop(0, ROWS, dots0, (zero, zero), unroll=16)
 
     def beside1():
         dot_start(0, 1, dot_finish(0, 0))
+
+    def background():
         g0_copy().wait_recv()
         split_pairs(g0_recv, g0_w, FACE * 3 // 2)
 
+    def nothing():
+        pass
+
     def beside2():
         dot_start(1, 1, dot_finish(1, 0))
 
-    later_product(1, m0, n0, beside1)
+    later_product(1, m0, n0, lambda: dot_start(0, 0, dot_pack(*sums0)), beside1, background)
     gam0, del0 = dot_unpack(dot_finish(0, 1))
     alpha0 = gam0 / del0
     al0 = jnp.broadcast_to(alpha0, (RHS, 128))
@@ -502,9 +520,9 @@
 
     sums = lax.fori_loop(3 * FACE, ROWS, update0, (zero, zero), unroll=16)
     send_top(8, w1)
-    dot_start(1, 0, dot_pack(*lax.fori_loop(0, 3 * FACE, update0, sums, unroll=16)))
-
-    later_product(2, m1, n1, beside2)
+    sums1 = lax.fori_loop(0, 3 * FACE, update0, sums, unroll=16)
+
+    later_product(2, m1, n1, lambda: dot_start(1, 0, dot_pack(*sums1)), beside2, nothing)
     gam1, del1 = dot_unpack(dot_finish(1, 1))
     beta1 = gam1 / gam0
     alpha1 = gam1 / (del1 - beta1 * gam1 / alpha0)

time: 70.3 us -> 64.6 us (0.919)
  Pallas kernels: 69.3 us -> 63.6 us
    pallas_call x1, Pallas kernels: 66.3 us -> 60.6 us  [body(): pl.pallas_call(kernel, out_shape=(jax.ShapeDtypeStruct((6, ROWS // 2, RHS...]
where the time goes in v4:
time: 64.6 us; the launch traced here: 64.5 us
  Pallas kernels  63.6 us (98%)
  between operations  0.82 us (1%)
    pallas_call x1, Pallas kernels, body(): pl.pallas_call(kernel, out_shape=(jax.ShapeDtypeStruct((6, ROWS // 2, RHS...  60.6 us
    pallas_call x1, Pallas kernels, body(): pl.pallas_call(finish, out_shape=(out, out), in_specs=[hbm, hbm], out_spe...  3.01 us

profile of v4, /device:TPU:1, one launch (start us, length us, event | category | flops | bytes accessed | tf_op | source)
XLA Modules:
  0.0 64.5 jit_solution(11177547408667954781)
XLA Ops:
  0.6 60.6 %shard_map.77 = (f32[6,32,32,128]{3,2,1,0:T(8,128)}, f32[2,32,128]{2,1,0:T(8,128)}) custom-call(f32[64,32,64]{2,1,0:T(8,128)} %rhs_hbm.1, f32[64,7,64,64]{3,2,1,0:T(8,128)} %a_hbm.1, f32[64,4,64,64]{3,2,1,0:T(8,128)} %g_hbm.1, s32[6,64]{1,0:T(8,128)} %bitcast.1, s32[1,16]{1,0:T(1,128)} %send_up.1, s32[1,16]{1,0:T(1,128)} %send_down.1), custom_call_target="tpu_custom_call" | custom-call | tf_op jit(solution)/shard_map/pallas_call | solution.py:618
  61.3 3.0 %shard_map.78 = (f32[64,32,64]{2,1,0:T(8,128)}, f32[64,32,64]{2,1,0:T(8,128)}) custom-call(f32[6,32,32,128]{3,2,1,0:T(8,128)} %get-tuple-element.4.parts_hbm, f32[2,32,128]{2,1,0:T(8,128)} %get-tuple-element.5.coef_hbm), custom_call_target="tpu_custom_call" | custom-call | tf_op jit(solution)/shard_map/pallas_call | solution.py:659

commit v5 on v4

--- a/solution.py
+++ b/solution.py
@@ -19,8 +19,8 @@
 G_CHUNK = 16
 A_CHUNK = 8
 A_SLOTS = 4
-GROUPS = (((1, 2), (2, 4), (64, 4)), ((8, 8),))
-FIRST_SLOT = (0, 31, 38)
+GROUPS = (((1, 2), (8, 8)), ((2, 4), (64, 4)))
+FIRST_SLOT = (0, 15, 30)
 LAST_CHUNKS = 4
 
 
@@ -305,10 +305,10 @@
         def part_low(h):
             out_m[h] = times_transposed([packed_y[h + FACE]], [g_w[place[h + FACE] * 4 + 3]])
 
+        start_sum()
         loop(3 * FACE, ROWS, inner_y)
         loop(0, FACE, part_high)
         send_top(base + 2, out_m)
-        start_sum()
         loop(0, FACE, bottom)
         send_bottom(base + 1, y_loc)
         loop(FACE, 2 * FACE, inner_y)

time: 64.6 us -> 63.2 us (0.978)
  Pallas kernels: 63.6 us -> 62.2 us
    pallas_call x1, Pallas kernels: 60.6 us -> 59.2 us  [body(): pl.pallas_call(kernel, out_shape=(jax.ShapeDtypeStruct((6, ROWS // 2, RHS...]
where the time goes in v5:
time: 63.2 us; the launch traced here: 63 us
  Pallas kernels  62.2 us (98%)
  between operations  0.82 us (1%)
    pallas_call x1, Pallas kernels, body(): pl.pallas_call(kernel, out_shape=(jax.ShapeDtypeStruct((6, ROWS // 2, RHS...  59.2 us
    pallas_call x1, Pallas kernels, body(): pl.pallas_call(finish, out_shape=(out, out), in_specs=[hbm, hbm], out_spe...  3.01 us

profile of v5, /device:TPU:1, one launch (start us, length us, event | category | flops | bytes accessed | tf_op | source)
XLA Modules:
  0.0 63.0 jit_solution(16588515139871000259)
XLA Ops:
  0.6 59.2 %shard_map.77 = (f32[6,32,32,128]{3,2,1,0:T(8,128)}, f32[2,32,128]{2,1,0:T(8,128)}) custom-call(f32[64,32,64]{2,1,0:T(8,128)} %rhs_hbm.1, f32[64,7,64,64]{3,2,1,0:T(8,128)} %a_hbm.1, f32[64,4,64,64]{3,2,1,0:T(8,128)} %g_hbm.1, s32[6,64]{1,0:T(8,128)} %bitcast.1, s32[1,16]{1,0:T(1,128)} %send_up.1, s32[1,16]{1,0:T(1,128)} %send_down.1), custom_call_target="tpu_custom_call" | custom-call | tf_op jit(solution)/shard_map/pallas_call | solution.py:618
  59.9 3.0 %shard_map.78 = (f32[64,32,64]{2,1,0:T(8,128)}, f32[64,32,64]{2,1,0:T(8,128)}) custom-call(f32[6,32,32,128]{3,2,1,0:T(8,128)} %get-tuple-element.4.parts_hbm, f32[2,32,128]{2,1,0:T(8,128)} %get-tuple-element.5.coef_hbm), custom_call_target="tpu_custom_call" | custom-call | tf_op jit(solution)/shard_map/pallas_call | solution.py:659
